TPU v7x, 512 devices: a whole 4x4x16 slice. The times are simulated.
512 devices in a mesh: prow: 32 (over z, core), pcol: 16 (over y, x).
Axes of the slice: x: 4, y: 4, z: 16, core: 2. Of those that a mesh axis runs over, the one named last changes fastest.
Arguments:
- rhs: float32 [4, 32, 16, 64, 128], P(None, 'prow', 'pcol'), may hold values from -6 to 6
- l_inverse: float32 [4, 32, 16, 128, 128], P(None, 'prow', 'pcol'), may hold values from -0.15 to 1.5
- u_inverse: float32 [4, 32, 16, 128, 128], P(None, 'prow', 'pcol'), may hold values from -0.15 to 1.5
- l_tiles: float32 [3, 32, 16, 16, 64, 128], P(None, 'prow', 'pcol'), may hold values from -0.125 to 0.125
- l_source: int32 [3, 32, 16, 16], P(None, 'prow', 'pcol'), may hold values from 0 to 31, as said below
- l_target: int32 [3, 32, 16, 16], P(None, 'prow', 'pcol'), may hold values from 0 to 15, as said below
- l_rows: int32 [3, 32, 16, 16, 64], P(None, 'prow', 'pcol'), may hold values from 0 to 127, as said below
- u_tiles: float32 [3, 32, 16, 16, 64, 128], P(None, 'prow', 'pcol'), may hold values from -0.125 to 0.125
- u_source: int32 [3, 32, 16, 16], P(None, 'prow', 'pcol'), may hold values from 0 to 31, as said below
- u_target: int32 [3, 32, 16, 16], P(None, 'prow', 'pcol'), may hold values from 0 to 15, as said below
- u_cols: int32 [3, 32, 16, 16, 64], P(None, 'prow', 'pcol'), may hold values from 0 to 127, as said below
Outputs:
- solution: float32 [4, 32, 16, 64, 128], P(None, 'prow', 'pcol')
Inputs may be any that keep to these rules, and one draw needn't show every extreme that they name: Within one device and level the 16 pairs (l_source, l_target) are distinct; over all devices each pair of a source process row and a target process column occurs 16 times a level. `l_target`: see l_source. `l_rows`: distinct and increasing within a tile. The structure of U is that of L transposed: U tile k of a level on device (r, c) belongs to L tile k of that level on device (u_source, u_target), whose l_source is r and l_target is c. `u_target`: see u_source. `u_cols`: equal to the l_rows of the L tile that the U tile belongs to.
All inputs are finite; a program needn't handle non-finite values.
Results may differ from a plain program's by a relative error of at most 0.0001.
Values sent between devices are 32-bit elements; how exact they have to be, the bound alone decides.
No kernel may reach another device: no remote copies, remote signals or barrier semaphores. Data moves between devices by JAX's collectives and lax.ppermute only.
A program may use at most 64 MiB of HBM per device.

v0:
```python
import jax
import jax.numpy as jnp
from jax import lax
from jax.sharding import PartitionSpec as P


def apply_inverse(vectors, inverse):
    return jnp.einsum("nj,ij->ni", vectors, inverse, precision=lax.Precision.HIGHEST)


def dense_tiles(tiles, structure, block_width):
    positions = lax.broadcasted_iota(jnp.int32, (1, 1, block_width), 2)
    placement = (structure[:, :, None] == positions).astype(jnp.float32)
    return jnp.einsum("tij,tib->tjb", placement, tiles, precision=lax.Precision.HIGHEST)


def solve_columns(
    rhs,
    l_inverse,
    u_inverse,
    l_tiles,
    l_source,
    l_target,
    l_rows,
    u_tiles,
    u_source,
    u_target,
    u_cols,
):
    level_count = rhs.shape[0]
    column_rows = rhs.shape[1]
    block_width = rhs.shape[2]
    col_count = lax.axis_size("pcol")
    slot_ids = jnp.arange(col_count, dtype=jnp.int32)
    forward = [apply_inverse(rhs[0], l_inverse[0])]
    for level_index in range(1, level_count):
        section = level_index - 1
        gathered = lax.all_gather(forward[-1][None], "prow", axis=0, tiled=True)
        blocks = gathered[l_source[section]]
        full_tiles = dense_tiles(l_tiles[section], l_rows[section], block_width)
        products = jnp.einsum("tnb,tjb->tnj", blocks, full_tiles, precision=lax.Precision.HIGHEST)
        onehot = (l_target[section][:, None] == slot_ids[None, :]).astype(jnp.float32)
        partial_value = jnp.einsum("tnj,tc->ncj", products, onehot, precision=lax.Precision.HIGHEST)
        partial_value = partial_value.reshape(column_rows, col_count * block_width)
        reduced = lax.psum_scatter(partial_value, "pcol", scatter_dimension=1, tiled=True)
        forward.append(apply_inverse(rhs[level_index] - reduced, l_inverse[level_index]))
    current = apply_inverse(forward[-1], u_inverse[level_count - 1])
    result = [current]
    for level_index in range(level_count - 2, -1, -1):
        gathered = lax.all_gather(current[None], "prow", axis=0, tiled=True)
        blocks = gathered[u_source[level_index]]
        full_tiles = dense_tiles(u_tiles[level_index], u_cols[level_index], block_width)
        products = jnp.einsum("tnj,tjb->tnb", blocks, full_tiles, precision=lax.Precision.HIGHEST)
        onehot = (u_target[level_index][:, None] == slot_ids[None, :]).astype(jnp.float32)
        partial_value = jnp.einsum("tnb,tc->ncb", products, onehot, precision=lax.Precision.HIGHEST)
        partial_value = partial_value.reshape(column_rows, col_count * block_width)
        reduced = lax.psum_scatter(partial_value, "pcol", scatter_dimension=1, tiled=True)
        current = apply_inverse(forward[level_index] - reduced, u_inverse[level_index])
        result.append(current)
    return jnp.stack(result[::-1])


def body(
    rhs,
    l_inverse,
    u_inverse,
    l_tiles,
    l_source,
    l_target,
    l_rows,
    u_tiles,
    u_source,
    u_target,
    u_cols,
):
    local_rhs = rhs[:, 0, 0]
    factors = (
        l_inverse[:, 0, 0],
        u_inverse[:, 0, 0],
        l_tiles[:, 0, 0],
        l_source[:, 0, 0],
        l_target[:, 0, 0],
        l_rows[:, 0, 0],
        u_tiles[:, 0, 0],
        u_source[:, 0, 0],
        u_target[:, 0, 0],
        u_cols[:, 0, 0],
    )
    solution = solve_columns(local_rhs, *factors)
    return solution[:, None, None]


def solution(mesh):
    in_specs = (
        P(None, "prow", "pcol", None, None),
        P(None, "prow", "pcol", None, None),
        P(None, "prow", "pcol", None, None),
        P(None, "prow", "pcol", None, None, None),
        P(None, "prow", "pcol", None),
        P(None, "prow", "pcol", None),
        P(None, "prow", "pcol", None, None),
        P(None, "prow", "pcol", None, None, None),
        P(None, "prow", "pcol", None),
        P(None, "prow", "pcol", None),
        P(None, "prow", "pcol", None, None),
    )
    out_specs = P(None, "prow", "pcol", None, None)
    return jax.shard_map(body, mesh=mesh, in_specs=in_specs, out_specs=out_specs, check_vma=False)
```

profile of v0, /device:TPU:2, one launch (start us, length us, event | category | flops | bytes accessed | tf_op | source)
XLA Modules:
  0.0 995.3 jit_solution(4750612807057358345)
XLA Ops:
  6.5 1.7 fusion.49
  8.3 0.0 reduce-scatter.7.cloned.1.call-start
  8.3 1.2 fusion.87
  9.5 1.2 slice_bitcast_fusion.6
  10.8 0.7 slice_bitcast_fusion.3
  11.5 2.2 fusion.10
  13.7 70.9 %all-gather.13.cloned.1.call-done = f32[2048,128]{1,0:T(8,128)} async-done(((f32[64,128]{1,0:T(8,128)}), f32[2048,128]{1,0:T(8,128)}) %all-gather.13.cloned.1.call-update) | async-done | bytes 1048592 | tf_op jit(solution)/shard_map/all_gather | solution.py:38
  84.6 1.8 gather_fusion
  86.4 2.1 fusion.91
  88.6 0.7 fusion.22
  89.3 1.0 copy.48
  90.3 0.0 all-gather.15.cloned.1.call-start
  90.3 84.5 %reduce-scatter.7.cloned.1.call-done = f32[64,128]{1,0:T(8,128)} async-done(((f32[64,2048]{1,0:T(8,128)}), f32[64,128]{1,0:T(8,128)}) %reduce-scatter.7.cloned.1.call-update) | async-done | bytes 32784 | tf_op jit(solution)/shard_map/reduce_scatter | solution.py:45
  174.9 1.6 fusion.47
  176.5 0.0 reduce-scatter.9.cloned.1.call-start
  176.6 1.2 fusion.8
  177.8 69.9 %all-gather.15.cloned.1.call-done = f32[2048,128]{1,0:T(8,128)} async-done(((f32[64,128]{1,0:T(8,128)}), f32[2048,128]{1,0:T(8,128)}) %all-gather.15.cloned.1.call-update) | async-done | bytes 1048592 | tf_op jit(solution)/shard_map/all_gather | solution.py:38
  247.7 1.8 gather_fusion.1
  249.5 2.1 fusion.92
  251.6 0.7 fusion.20
  252.3 1.0 copy.47
  253.3 0.0 all-gather.17.cloned.1.call-start
  253.4 84.5 %reduce-scatter.9.cloned.1.call-done = f32[64,128]{1,0:T(8,128)} async-done(((f32[64,2048]{1,0:T(8,128)}), f32[64,128]{1,0:T(8,128)}) %reduce-scatter.9.cloned.1.call-update) | async-done | bytes 32784 | tf_op jit(solution)/shard_map/reduce_scatter | solution.py:45
  337.9 1.6 fusion.45
  339.5 0.0 reduce-scatter.11.cloned.1.call-start
  339.6 1.2 fusion.6
  340.8 69.5 %all-gather.17.cloned.1.call-done = f32[2048,128]{1,0:T(8,128)} async-done(((f32[64,128]{1,0:T(8,128)}), f32[2048,128]{1,0:T(8,128)}) %all-gather.17.cloned.1.call-update) | async-done | bytes 1048592 | tf_op jit(solution)/shard_map/all_gather | solution.py:38
  410.3 1.8 gather_fusion.2
  412.1 2.1 fusion.93
  414.3 0.7 fusion.18
  415.0 1.0 copy.46
  416.0 0.0 all-gather.19.cloned.1.call-start
  416.0 84.5 %reduce-scatter.11.cloned.1.call-done = f32[64,128]{1,0:T(8,128)} async-done(((f32[64,2048]{1,0:T(8,128)}), f32[64,128]{1,0:T(8,128)}) %reduce-scatter.11.cloned.1.call-update) | async-done | bytes 32784 | tf_op jit(solution)/shard_map/reduce_scatter | solution.py:45
  500.6 1.0 fusion.43
  501.6 1.7 fusion.41
  503.3 0.2 reduce-scatter.13.cloned.1.call-start
  503.6 1.2 fusion.4
  504.8 69.1 %all-gather.19.cloned.1.call-done = f32[2048,128]{1,0:T(8,128)} async-done(((f32[64,128]{1,0:T(8,128)}), f32[2048,128]{1,0:T(8,128)}) %all-gather.19.cloned.1.call-update) | async-done | bytes 1048592 | tf_op jit(solution)/shard_map/all_gather | solution.py:50
  573.9 1.8 gather_fusion.3
  575.7 1.1 fusion.94
  576.8 0.7 fusion.16
  577.4 1.0 copy.45
  578.4 0.0 all-gather.21.cloned.1.call-start
  578.5 84.6 %reduce-scatter.13.cloned.1.call-done = f32[64,128]{1,0:T(8,128)} async-done(((f32[64,2048]{1,0:T(8,128)}), f32[64,128]{1,0:T(8,128)}) %reduce-scatter.13.cloned.1.call-update) | async-done | bytes 32784 | tf_op jit(solution)/shard_map/reduce_scatter | solution.py:57
  663.0 1.6 fusion.39
  664.7 0.0 reduce-scatter.15.cloned.1.call-start
  664.7 1.2 fusion.2
  665.9 69.7 %all-gather.21.cloned.1.call-done = f32[2048,128]{1,0:T(8,128)} async-done(((f32[64,128]{1,0:T(8,128)}), f32[2048,128]{1,0:T(8,128)}) %all-gather.21.cloned.1.call-update) | async-done | bytes 1048592 | tf_op jit(solution)/shard_map/all_gather | solution.py:50
  735.6 1.8 gather_fusion.4
  737.4 1.1 fusion.95
  738.5 0.7 fusion.14
  739.2 1.0 copy.44
  740.2 84.5 %reduce-scatter.15.cloned.1.call-done = f32[64,128]{1,0:T(8,128)} async-done(((f32[64,2048]{1,0:T(8,128)}), f32[64,128]{1,0:T(8,128)}) %reduce-scatter.15.cloned.1.call-update) | async-done | bytes 32784 | tf_op jit(solution)/shard_map/reduce_scatter | solution.py:57
  824.8 1.6 fusion.37
  826.4 0.0 reduce-scatter.17.cloned.1.call-start
  826.5 1.2 fusion
  827.6 69.9 %all-gather.23.cloned.1.call-done = f32[2048,128]{1,0:T(8,128)} async-done(((f32[64,128]{1,0:T(8,128)}), f32[2048,128]{1,0:T(8,128)}) %all-gather.23.cloned.1.call-update) | async-done | bytes 1048592 | tf_op jit(solution)/shard_map/all_gather | solution.py:50
  897.6 1.8 gather_fusion.5
  899.4 1.1 fusion.96
  900.5 0.7 fusion.12
  901.2 1.0 copy.43
  902.1 84.6 %reduce-scatter.17.cloned.1.call-done = f32[64,128]{1,0:T(8,128)} async-done(((f32[64,2048]{1,0:T(8,128)}), f32[64,128]{1,0:T(8,128)}) %reduce-scatter.17.cloned.1.call-update) | async-done | bytes 32784 | tf_op jit(solution)/shard_map/reduce_scatter | solution.py:57
  986.8 1.0 convolution_bitcast_fusion
  987.8 0.7 maximum_bitcast_fusion
  (55 shorter events, 0.4 us)
Async XLA Ops:
  6.5 78.1 %all-gather.13.cloned.1.call-start = ((), (), s32[]{:S(2)}) async-start(), calls=%async_computation.12 | async-start | bytes 1081344 | tf_op jit(solution)/shard_map/all_gather | solution.py:38
  8.3 166.6 %reduce-scatter.7.cloned.1.call-start = ((), (), s32[]{:S(2)}) async-start(), calls=%async_computation.6 | async-start | bytes 557056 | tf_op jit(solution)/shard_map/reduce_scatter | solution.py:45
  88.6 86.3 %copy-start.8 = (f32[4,1,1,128,128]{4,3,2,1,0:T(8,128)S(1)}, f32[4,1,1,128,128]{4,3,2,1,0:T(8,128)}, u32[]{:S(2)}) copy-start(f32[4,1,1,128,128]{4,3,2,1,0:T(8,128)} %param.12) | copy-start | bytes 786436
  88.6 86.3 %copy-start.10 = (f32[4,1,1,64,128]{4,3,2,1,0:T(8,128)S(1)}, f32[4,1,1,64,128]{4,3,2,1,0:T(8,128)}, u32[]{:S(2)}) copy-start(f32[4,1,1,64,128]{4,3,2,1,0:T(8,128)} %param.11) | copy-start | bytes 393220
  88.6 88.0 %copy-start = (f32[3,1,1,16,64,128]{5,4,3,2,1,0:T(8,128)S(1)}, f32[3,1,1,16,64,128]{5,4,3,2,1,0:T(8,128)}, u32[]{:S(2)}) copy-start(f32[3,1,1,16,64,128]{5,4,3,2,1,0:T(8,128)} %param.14) | copy-start | bytes 4718596
  90.3 157.4 %all-gather.15.cloned.1.call-start = ((), (), s32[]{:S(2)}) async-start(), calls=%async_computation.13 | async-start | bytes 1081344 | tf_op jit(solution)/shard_map/all_gather | solution.py:38
  176.5 161.4 %reduce-scatter.9.cloned.1.call-start = ((), (), s32[]{:S(2)}) async-start(), calls=%async_computation.7 | async-start | bytes 557056 | tf_op jit(solution)/shard_map/reduce_scatter | solution.py:45
  249.5 2.2 copy-start.12
  251.6 88.0 %copy-start.13 = (s32[16]{0:T(128)S(1)}, s32[16]{0:T(128)}, u32[]{:S(2)}) copy-start(s32[16]{0:T(128)} %get-tuple-element.20) | copy-start | bytes 196
  253.3 157.0 %all-gather.17.cloned.1.call-start = ((), (), s32[]{:S(2)}) async-start(), calls=%async_computation.14 | async-start | bytes 1081344 | tf_op jit(solution)/shard_map/all_gather | solution.py:38
  339.5 161.0 %reduce-scatter.11.cloned.1.call-start = ((), (), s32[]{:S(2)}) async-start(), calls=%async_computation.8 | async-start | bytes 557056 | tf_op jit(solution)/shard_map/reduce_scatter | solution.py:45
  414.3 89.3 %copy-start.14 = (s32[3,1,1,16]{3,2,1,0:T(1,128)S(1)}, s32[3,1,1,16]{3,2,1,0:T(1,128)}, u32[]{:S(2)}) copy-start(s32[3,1,1,16]{3,2,1,0:T(1,128)} %param.19) | copy-start | bytes 580
  414.3 89.3 %copy-start.15 = (s32[3,1,1,16]{3,2,1,0:T(1,128)S(1)}, s32[3,1,1,16]{3,2,1,0:T(1,128)}, u32[]{:S(2)}) copy-start(s32[3,1,1,16]{3,2,1,0:T(1,128)} %param.20) | copy-start | bytes 580
  414.3 89.3 %copy-start.11 = (s32[3,1,1,16,64]{4,3,2,1,0:T(8,128)S(1)}, s32[3,1,1,16,64]{4,3,2,1,0:T(8,128)}, u32[]{:S(2)}) copy-start(s32[3,1,1,16,64]{4,3,2,1,0:T(8,128)} %param.21) | copy-start | bytes 36868
  414.3 89.3 %copy-start.1 = (f32[3,1,1,16,64,128]{5,4,3,2,1,0:T(8,128)S(1)}, f32[3,1,1,16,64,128]{5,4,3,2,1,0:T(8,128)}, u32[]{:S(2)}) copy-start(f32[3,1,1,16,64,128]{5,4,3,2,1,0:T(8,128)} %param.18) | copy-start | bytes 4718596
  416.0 157.9 %all-gather.19.cloned.1.call-start = ((), (), s32[]{:S(2)}) async-start(), calls=%async_computation.15 | async-start | bytes 1081344 | tf_op jit(solution)/shard_map/all_gather | solution.py:50
  503.3 159.7 %reduce-scatter.13.cloned.1.call-start = ((), (), s32[]{:S(2)}) async-start(), calls=%async_computation.9 | async-start | bytes 557056 | tf_op jit(solution)/shard_map/reduce_scatter | solution.py:57
  576.7 86.3 %copy-start.3 = (f32[64,128]{1,0:T(8,128)S(1)}, f32[64,128]{1,0:T(8,128)}, u32[]{:S(2)}) copy-start(f32[64,128]{1,0:T(8,128)} %fusion.45) | copy-start | bytes 98308
  576.7 86.3 %copy-start.9 = (f32[4,1,1,128,128]{4,3,2,1,0:T(8,128)S(1)}, f32[4,1,1,128,128]{4,3,2,1,0:T(8,128)}, u32[]{:S(2)}) copy-start(f32[4,1,1,128,128]{4,3,2,1,0:T(8,128)} %param.13) | copy-start | bytes 786436
  578.4 157.2 %all-gather.21.cloned.1.call-start = ((), (), s32[]{:S(2)}) async-start(), calls=%async_computation.16 | async-start | bytes 1081344 | tf_op jit(solution)/shard_map/all_gather | solution.py:50
  664.7 160.1 %reduce-scatter.15.cloned.1.call-start = ((), (), s32[]{:S(2)}) async-start(), calls=%async_computation.10 | async-start | bytes 557056 | tf_op jit(solution)/shard_map/reduce_scatter | solution.py:57
  738.5 86.3 %copy-start.2 = (f32[64,128]{1,0:T(8,128)S(1)}, f32[64,128]{1,0:T(8,128)}, u32[]{:S(2)}) copy-start(f32[64,128]{1,0:T(8,128)} %fusion.47) | copy-start | bytes 98308
  740.2 157.4 %all-gather.23.cloned.1.call-start = ((), (), s32[]{:S(2)}) async-start(), calls=%async_computation.17 | async-start | bytes 1081344 | tf_op jit(solution)/shard_map/all_gather | solution.py:50
  826.4 160.4 %reduce-scatter.17.cloned.1.call-start = ((), (), s32[]{:S(2)}) async-start(), calls=%async_computation.11 | async-start | bytes 557056 | tf_op jit(solution)/shard_map/reduce_scatter | solution.py:57
  900.4 86.3 %copy-start.4 = (f32[64,128]{1,0:T(8,128)S(1)}, f32[64,128]{1,0:T(8,128)}, u32[]{:S(2)}) copy-start(f32[64,128]{1,0:T(8,128)} %fusion.49) | copy-start | bytes 98308
  900.4 87.3 %copy-start.5 = (f32[64,128]{1,0:T(8,128)S(1)}, f32[64,128]{1,0:T(8,128)}, u32[]{:S(2)}) copy-start(f32[64,128]{1,0:T(8,128)} %fusion.39) | copy-start | bytes 98308
  900.5 87.3 %copy-start.6 = (f32[64,128]{1,0:T(8,128)S(1)}, f32[64,128]{1,0:T(8,128)}, u32[]{:S(2)}) copy-start(f32[64,128]{1,0:T(8,128)} %fusion.37) | copy-start | bytes 98308
  900.5 87.3 %copy-start.7 = (f32[64,128]{1,0:T(8,128)S(1)}, f32[64,128]{1,0:T(8,128)}, u32[]{:S(2)}) copy-start(f32[64,128]{1,0:T(8,128)} %fusion.41) | copy-start | bytes 98308
Sparse Core Ops, SparseCore 0:
  9.5 75.1 all-gather.12
  90.4 84.4 reduce-scatter.6
  177.2 70.4 all-gather.14
  253.4 84.4 reduce-scatter.8
  339.9 70.4 all-gather.16
  416.1 84.4 reduce-scatter.10
  503.4 70.4 all-gather.18
  578.5 84.4 reduce-scatter.12
  665.2 70.4 all-gather.20
  740.3 84.4 reduce-scatter.14
  827.1 70.4 all-gather.22
  902.3 84.4 reduce-scatter.16
where the time goes:
time: 996 us; the launch traced here: 995 us
  waiting for transfers between devices  927 us (93%)
  matrix products  33.5 us (3%)
  local copies, waits for them, and re-layouts  18.7 us (2%)
  between operations  14 us (1%)
    reduce_scatter x6, waiting for transfers between devices, solve_columns(): lax.psum_scatter(partial_value, 'pcol', scatter_dimension=1, tiled=True)  507 us
    all_gather x3, waiting for transfers between devices, solve_columns(): gathered = lax.all_gather(forward[-1][None], 'prow', axis=0, tiled=True)  210 us
    all_gather x3, waiting for transfers between devices, solve_columns(): gathered = lax.all_gather(current[None], 'prow', axis=0, tiled=True)  209 us
  transfers between devices with their start and end apart: 12, of which 12 were waited for; matrix products, arithmetic and copies ran while one was open for 1% of the time, Pallas kernels for 0%

commit v1 on v0

v1 whole, which is shorter than its diff:
```python
import jax
import jax.numpy as jnp
from jax import lax
from jax.experimental import pallas as pl
from jax.experimental.pallas import tpu as pltpu
from jax.sharding import PartitionSpec as P

F32 = jnp.float32
BF16 = jnp.bfloat16
VMEM_LIMIT = 48 * 1024 * 1024


def dot_nt(a, b):
    return lax.dot_general(a, b, (((1,), (1,)), ((), ())), preferred_element_type=F32)


def dot_nn(a, b):
    return lax.dot_general(a, b, (((1,), (0,)), ((), ())), preferred_element_type=F32)


def split(x):
    high = x.astype(BF16)
    low = (x - high.astype(F32)).astype(BF16)
    return jnp.concatenate([high, low], axis=0)


def fold(x):
    half = x.shape[0] // 2
    return x[:half] + x[half:]


def apply_inverse(vectors, inverse):
    size = inverse.shape[0]
    out = fold(dot_nt(split(vectors), split(inverse)))
    return out[:, :size] + out[:, size:]


def structure_matrix(rows):
    positions = lax.broadcasted_iota(jnp.int32, (128, rows.shape[1]), 0)
    return jnp.where(positions == rows, 1.0, 0.0).astype(BF16)


def products_kernel(transposed, offset, source_ref, target_ref, rows_ref, blocks_ref, own_ref, oth_ref, out_ref, parts_ref):
    tiles = own_ref.shape[0]
    for first in range(0, 2 * tiles, 8):
        group = range(first, first + 8)
        held = []
        for t in group:
            block = split(blocks_ref[source_ref[offset + t]])
            tile = split((own_ref if t < tiles else oth_ref)[t % tiles])
            places = structure_matrix(rows_ref[t : t + 1, :])
            if transposed:
                held.append((fold(dot_nt(block, tile)), places))
            else:
                held.append((dot_nn(block, places).astype(BF16), tile))
        for t, (left, right) in zip(group, held):
            if transposed:
                parts_ref[t] = fold(dot_nt(split(left), right))
            else:
                parts_ref[t] = fold(dot_nn(left, right))
    out_ref[...] = jnp.zeros_like(out_ref)
    for t in range(2 * tiles):
        out_ref[target_ref[offset + t], t // tiles] += parts_ref[t]


def products(transposed, offset, level, oth_level, source, target, rows, blocks, own, oth):
    tiles = own.shape[1]
    cols, half, width = 16, blocks.shape[1], blocks.shape[2]
    spec = lambda at: pl.BlockSpec((None,) + own.shape[1:], lambda i: (at, 0, 0, 0))
    smem = pl.BlockSpec(memory_space=pltpu.SMEM)
    flops = 2 * tiles * 2 * 2 * (2 * half) * 128 * 128
    return pl.pallas_call(
        lambda *refs: products_kernel(transposed, offset, *refs),
        grid=(1,),
        out_shape=jax.ShapeDtypeStruct((cols, 2, half, width), F32),
        in_specs=[
            smem,
            smem,
            pl.BlockSpec((None,) + rows.shape[1:], lambda i: (offset // (2 * tiles), 0, 0)),
            pl.BlockSpec(blocks.shape, lambda i: (0, 0, 0)),
            spec(level),
            spec(oth_level),
        ],
        out_specs=pl.BlockSpec((cols, 2, half, width), lambda i: (0, 0, 0, 0)),
        scratch_shapes=[pltpu.VMEM((2 * tiles, half, width), F32)],
        compiler_params=pltpu.CompilerParams(vmem_limit_bytes=VMEM_LIMIT),
        cost_estimate=pl.CostEstimate(flops=flops, bytes_accessed=2 << 20, transcendentals=0),
    )(source, target, rows, blocks, own, oth)


def solve_kernel(then_upper, parts_ref, start_own_ref, start_oth_ref, own_ref, oth_ref, *rest):
    if then_upper:
        up_own_ref, up_oth_ref, mid_ref, out_ref = rest
    else:
        (out_ref,) = rest
    total = parts_ref[0]
    for k in range(1, parts_ref.shape[0]):
        total = total + parts_ref[k]
    for s, (start_ref, inv_ref) in enumerate(((start_own_ref, own_ref), (start_oth_ref, oth_ref))):
        value = apply_inverse(start_ref[...] - total[s], inv_ref[...])
        if then_upper:
            mid_ref[s] = value
            value = apply_inverse(value, (up_own_ref, up_oth_ref)[s][...])
        out_ref[s] = value


def pick(array, *at):
    tail = array.shape[len(at) :]
    return pl.BlockSpec((None,) * len(at) + tail, lambda i: tuple(at) + (0,) * len(tail))


def solve(parts, *operands, then_upper=False):
    shape = jax.ShapeDtypeStruct(parts.shape[1:], F32)
    whole = pl.BlockSpec(shape.shape, lambda i: (0, 0, 0))
    outs = 2 if then_upper else 1
    result = pl.pallas_call(
        lambda *refs: solve_kernel(then_upper, *refs),
        grid=(1,),
        out_shape=[shape] * outs,
        in_specs=[pl.BlockSpec(parts.shape, lambda i: (0, 0, 0, 0))] + [pick(*op) for op in operands],
        out_specs=[whole] * outs,
        compiler_params=pltpu.CompilerParams(vmem_limit_bytes=VMEM_LIMIT),
        cost_estimate=pl.CostEstimate(flops=1 << 24, bytes_accessed=1 << 20, transcendentals=0),
    )(parts, *[op[0] for op in operands])
    return result if then_upper else result[0]


def first_kernel(rhs_ref, inv_ref, out_ref):
    out_ref[...] = apply_inverse(rhs_ref[...], inv_ref[...])


def first_solve(rhs, inverse):
    return pl.pallas_call(
        first_kernel,
        grid=(1,),
        out_shape=jax.ShapeDtypeStruct(rhs.shape[1:], F32),
        in_specs=[pick(rhs, 0), pick(inverse, 0)],
        out_specs=pl.BlockSpec(rhs.shape[1:], lambda i: (0, 0)),
        compiler_params=pltpu.CompilerParams(vmem_limit_bytes=VMEM_LIMIT),
    )(rhs, inverse)


def body(rhs, l_inverse, u_inverse, l_tiles, l_source, l_target, l_rows, u_tiles, u_source, u_target, u_cols):
    rhs, l_inverse, u_inverse, l_tiles, l_source, l_target, l_rows, u_tiles, u_source, u_target, u_cols = (
        a[:, 0, 0] for a in (rhs, l_inverse, u_inverse, l_tiles, l_source, l_target, l_rows, u_tiles, u_source, u_target, u_cols)
    )
    levels, nrhs, width = rhs.shape
    steps = levels - 1
    tiles = l_tiles.shape[1]
    half = nrhs // 2
    prow = lax.axis_size("prow")
    pcol = lax.axis_size("pcol")
    parity = (lax.axis_index("prow") // 2) % 2
    pair = [(r, r ^ 2) for r in range(prow)]
    groups = [[4 * i + 2 * a + c for i in range(prow // 4) for c in range(2)] for a in range(2)]

    def swap(array):
        return lax.ppermute(array, "prow", pair)

    def halves(array):
        low, high = array[..., :half, :], array[..., half:, :]
        return jnp.where(parity == 0, low, high), jnp.where(parity == 0, high, low)

    def gather(value):
        got = lax.all_gather(value, "prow", axis=0, tiled=True, axis_index_groups=groups)
        return got.reshape(prow, half, width)

    def exchange(parts):
        return lax.all_to_all(parts, "pcol", 0, 0, tiled=True)

    mine, send = halves(first_solve(rhs, l_inverse))
    value = jnp.stack([mine, swap(send)])
    def packed(rows, source, target):
        return jnp.concatenate([rows, source[..., None], target[..., None]], axis=2)

    ints = jnp.stack([packed(l_rows, l_source, l_target), packed(u_cols, u_source, u_target)])
    ints = jnp.stack([ints, swap(ints)], axis=2).reshape(2 * steps, 2 * tiles, -1)
    rows = jnp.concatenate([ints[..., :-2], ints[..., :-2]], axis=2)
    raw = ints[..., -2].reshape(-1)
    source = (raw & ~3) + 2 * (raw & 1) + (((raw >> 1) & 1) ^ parity)
    target = ints[..., -1].reshape(-1)

    l_first = swap(l_tiles[:1])
    rhs_mine, rhs_send = halves(rhs[1:])
    rhs_oth = swap(rhs_send)
    l_inverse_oth = swap(l_inverse[1:])
    l_rest = swap(l_tiles[1:])
    u_inverse_oth = swap(u_inverse)
    u_oth = swap(u_tiles)

    forward = [value]
    result = None
    for level in range(1, levels):
        at = level - 1
        oth = (l_first, 0) if at == 0 else (l_rest, at - 1)
        parts = products(True, at * 2 * tiles, at, oth[1], source, target, rows, gather(value), l_tiles, oth[0])
        operands = [(rhs_mine, at), (rhs_oth, at), (l_inverse, level), (l_inverse_oth, at)]
        if level < levels - 1:
            value = solve(exchange(parts), *operands)
            forward.append(value)
        else:
            operands += [(u_inverse, level), (u_inverse_oth, level)]
            top, value = solve(exchange(parts), *operands, then_upper=True)
    result = [value]
    for level in range(levels - 2, -1, -1):
        offset = (steps + level) * 2 * tiles
        parts = products(False, offset, level, level, source, target, rows, gather(value), u_tiles, u_oth)
        start = forward[level]
        value = solve(exchange(parts), (start, 0), (start, 1), (u_inverse, level), (u_inverse_oth, level))
        result.append(value)
    result = jnp.stack(result[::-1])
    own, got = result[:, 0], swap(result[:, 1])
    solution = jnp.where(parity == 0, jnp.concatenate([own, got], axis=1), jnp.concatenate([got, own], axis=1))
    return solution[:, None, None]


def solution(mesh):
    spec = lambda tail: P(None, "prow", "pcol", *([None] * tail))
    in_specs = tuple(spec(n) for n in (2, 2, 2, 3, 1, 1, 2, 3, 1, 1, 2))
    return jax.shard_map(body, mesh=mesh, in_specs=in_specs, out_specs=spec(2), check_vma=False)
```

time: 996 us -> 341 us (0.34)
  the two profiles are of different devices: /device:TPU:2 before, /device:TPU:32 now
where the time goes in v1:
time: 341 us; the launch traced here: 340 us
  blocking collectives  239 us (70%)
  starting transfers between devices  41.2 us (12%)
  local copies, waits for them, and re-layouts  22.8 us (7%)
  Pallas kernels  17.5 us (5%)
  waiting for transfers between devices  16.8 us (5%)
    all_gather x6, blocking collectives, gather(): lax.all_gather(value, 'prow', axis=0, tiled=True, axis_index_groups=groups)  172 us
    all_to_all x4, blocking collectives, exchange(): return lax.all_to_all(parts, 'pcol', 0, 0, tiled=True)  67.1 us
    ppermute x9, starting transfers between devices, swap(): return lax.ppermute(array, 'prow', pair)  30.6 us
    unnamed x66, local copies, waits for them, and re-layouts  15.7 us
    pallas_call x6, Pallas kernels, products(): pl.pallas_call(lambda *refs: products_kernel(transposed, offset, *refs),...  13 us
    ppermute x9, waiting for transfers between devices, swap(): return lax.ppermute(array, 'prow', pair)  11.4 us
    all_to_all x2, starting transfers between devices, exchange(): return lax.all_to_all(parts, 'pcol', 0, 0, tiled=True)  10.7 us
  transfers between devices with their start and end apart: 11, of which 5 were waited for; matrix products, arithmetic and copies ran while one was open for 2% of the time, Pallas kernels for 3%

profile of v1, /device:TPU:32, one launch (start us, length us, event | category | flops | bytes accessed | tf_op | source)
XLA Modules:
  0.0 339.8 jit_solution(7154159543079388062)
XLA Ops:
  0.0 1.1 copy-done.2
  1.1 0.9 copy-done.26
  2.2 7.4 %collective-permute-start.1 = (f32[32,128]{1,0:T(8,128)S(1)}, f32[32,128]{1,0:T(8,128)S(1)}, u32[]{:S(2)}, u32[]{:S(2)}) collective-permute-start(f32[32,128]{1,0:T(8,128)S(1)} %get-tuple-element.16), channel_id=1, source_target_pairs={{0,32},{16,48},{32,0},{48,16},{64,96},{80,112},{96,64},{112,80},{1... | collective-permute-start | bytes 49160 | tf_op jit(solution)/shard_map/ppermute | solution.py:158
  9.6 0.8 copy.42
  10.3 0.8 copy.43
  11.1 0.8 copy.44
  11.9 0.8 copy.45
  12.6 0.8 add_bitcast_fusion
  13.5 1.9 collective-permute-start
  15.4 1.1 slice_bitcast_fusion.1
  16.5 3.9 %collective-permute-start.2 = (f32[1,16,64,128]{3,2,1,0:T(8,128)S(1)}, f32[1,16,64,128]{3,2,1,0:T(8,128)S(1)}, u32[]{:S(2)}, u32[]{:S(2)}) collective-permute-start(f32[1,16,64,128]{3,2,1,0:T(8,128)S(1)} %slice_bitcast_fusion.1), channel_id=1, source_target_pairs={{0,32},{16,48},{32,0},{48,16},{64,96},{80,112},{96,64},{112,80},{1... | collective-permute-start | bytes 1572872 | tf_op jit(solution)/shard_map/ppermute | solution.py:158
  20.5 0.7 slice_bitcast_fusion.2
  21.2 1.9 collective-permute-start.4
  23.1 1.1 slice_bitcast_fusion
  24.2 3.9 %collective-permute-start.5 = (f32[2,16,64,128]{3,2,1,0:T(8,128)}, f32[2,16,64,128]{3,2,1,0:T(8,128)}, u32[]{:S(2)}, u32[]{:S(2)}) collective-permute-start(f32[2,16,64,128]{3,2,1,0:T(8,128)} %slice_bitcast_fusion), channel_id=1, source_target_pairs={{0,32},{16,48},{32,0},{48,16},{64,96},{80,112},{96,64},{112,80},{1... | collective-permute-start | bytes 3145736 | tf_op jit(solution)/shard_map/ppermute | solution.py:158
  28.1 49.5 %all_gather.18.refs_3_ = f32[32,32,128]{2,1,0:T(8,128)} all-gather(f32[2,32,128]{2,1,0:T(8,128)S(1)} %pad_maximum_fusion.1.refs_1_.refs_2_), channel_id=1, replica_groups={{0,16,64,80,128,144,192,208,256,272,320,336,384,400,448,464},{32,48,96,..., dimensions={0}, use_global_device_ids=true | all-gather | bytes 557056 | tf_op jit(solution)/shard_map/all_gather | solution.py:165
  77.7 0.6 copy-done.14
  78.3 0.4 slice_reduce_fusion
  79.0 0.8 copy-done.20
  79.8 1.0 copy-done.13
  80.8 1.0 copy-done.21
  81.9 2.0 shard_map.110
  83.9 0.8 copy-done.12
  84.7 7.1 %all-to-all-start = ((f32[16,2,32,128]{3,2,1,0:T(8,128)}), f32[16,2,32,128]{3,2,1,0:T(8,128)}, u32[]{:S(2)}, u32[]{:S(2)}) async-start(f32[16,2,32,128]{3,2,1,0:T(8,128)} %copy-done.12), calls=%async_computation | async-start | bytes 1048576 | tf_op jit(solution)/shard_map/all_to_all | solution.py:169
  91.8 0.9 slice_bitcast_fusion.3
  92.7 3.1 collective-permute-start.3
  95.8 2.8 collective-permute-start.7
  98.7 0.6 copy-done.22
  99.4 4.6 %all-to-all-done.refs_0_ = f32[16,2,32,128]{3,2,1,0:T(8,128)} async-done(((f32[16,2,32,128]{3,2,1,0:T(8,128)}), f32[16,2,32,128]{3,2,1,0:T(8,128)}, u32[]{:S(2)}, u32[]{:S(2)}) %all-to-all-start) | async-done | bytes 524320 | tf_op jit(solution)/shard_map/all_to_all | solution.py:169
  103.9 0.8 copy-done.23
  104.7 1.2 shard_map.111.refs_1_.refs_2_
  106.0 44.2 %all_gather.19.refs_3_ = f32[32,32,128]{2,1,0:T(8,128)S(1)} all-gather(f32[2,32,128]{2,1,0:T(8,128)S(1)} %shard_map.111.refs_1_.refs_2_), channel_id=1, replica_groups={{0,16,64,80,128,144,192,208,256,272,320,336,384,400,448,464},{32,48,96,..., dimensions={0}, use_global_device_ids=true | all-gather | bytes 557056 | tf_op jit(solution)/shard_map/all_gather | solution.py:165
  150.2 2.5 shard_map.112
  152.7 19.1 %all_to_all.30.refs_0_ = f32[16,2,32,128]{3,2,1,0:T(8,128)S(1)} all-to-all(f32[16,2,32,128]{3,2,1,0:T(8,128)S(1)} %shard_map.112), channel_id=1, replica_groups=mesh['prow'=32,'pcol'=16] {'pcol'}, dimensions={0} | all-to-all | bytes 1048576 | tf_op jit(solution)/shard_map/all_to_all | solution.py:169
  171.8 1.0 shard_map.113.refs_1_.refs_2_
  172.8 17.6 %all_gather.20.refs_3_ = f32[32,32,128]{2,1,0:T(8,128)S(1)} all-gather(f32[2,32,128]{2,1,0:T(8,128)S(1)} %shard_map.113.refs_1_.refs_2_), channel_id=1, replica_groups={{0,16,64,80,128,144,192,208,256,272,320,336,384,400,448,464},{32,48,96,..., dimensions={0}, use_global_device_ids=true | all-gather | bytes 557056 | tf_op jit(solution)/shard_map/all_gather | solution.py:165
  190.4 0.6 copy-done.18
  191.1 2.5 shard_map.114
  193.6 0.8 copy-done.11
  194.4 3.6 %all-to-all-start.2 = ((f32[16,2,32,128]{3,2,1,0:T(8,128)}), f32[16,2,32,128]{3,2,1,0:T(8,128)S(1)}, u32[]{:S(2)}, u32[]{:S(2)}) async-start(f32[16,2,32,128]{3,2,1,0:T(8,128)} %copy-done.11), calls=%async_computation.2 | async-start | bytes 1048576 | tf_op jit(solution)/shard_map/all_to_all | solution.py:169
  198.0 3.8 %collective-permute-start.6 = (f32[4,128,128]{2,1,0:T(8,128)}, f32[4,128,128]{2,1,0:T(8,128)S(1)}, u32[]{:S(2)}, u32[]{:S(2)}) collective-permute-start(f32[4,128,128]{2,1,0:T(8,128)} %bitcast.60), channel_id=1, source_target_pairs={{0,32},{16,48},{32,0},{48,16},{64,96},{80,112},{96,64},{112,80},{1... | collective-permute-start | bytes 786440 | tf_op jit(solution)/shard_map/ppermute | solution.py:158
  201.7 7.0 %collective-permute-done.6.refs_6_.refs_4_ = f32[4,128,128]{2,1,0:T(8,128)S(1)} collective-permute-done((f32[4,128,128]{2,1,0:T(8,128)}, f32[4,128,128]{2,1,0:T(8,128)S(1)}, u32[]{:S(2)}, u32[]{:S(2)}) %collective-permute-start.6) | collective-permute-done | bytes 262176 | tf_op jit(solution)/shard_map/ppermute | solution.py:158
  208.7 0.7 copy-done.6
  209.5 0.8 all-to-all-done.2.refs_0_
  210.3 0.8 copy-done.9
  211.1 0.9 copy-done.4
  212.0 0.9 copy-done.7
  213.0 1.0 copy-done.10
  214.0 0.8 copy-done.25
  214.8 1.7 shard_map.115
  216.5 21.4 %all_gather.21.refs_3_ = f32[32,32,128]{2,1,0:T(8,128)S(1)} all-gather(f32[2,32,128]{2,1,0:T(8,128)S(1)} %get-tuple-element.6), channel_id=1, replica_groups={{0,16,64,80,128,144,192,208,256,272,320,336,384,400,448,464},{32,48,96,..., dimensions={0}, use_global_device_ids=true | all-gather | bytes 557056 | tf_op jit(solution)/shard_map/all_gather | solution.py:165
  237.9 0.7 copy-done.29
  238.6 0.6 copy-done.32
  239.2 2.0 shard_map.116
  241.2 18.0 %all_to_all.31.refs_0_ = f32[16,2,32,128]{3,2,1,0:T(8,128)S(1)} all-to-all(f32[16,2,32,128]{3,2,1,0:T(8,128)S(1)} %shard_map.116), channel_id=1, replica_groups=mesh['prow'=32,'pcol'=16] {'pcol'}, dimensions={0} | all-to-all | bytes 1048576 | tf_op jit(solution)/shard_map/all_to_all | solution.py:169
  259.4 17.7 %all_gather.22.refs_3_ = f32[32,32,128]{2,1,0:T(8,128)S(1)} all-gather(f32[2,32,128]{2,1,0:T(8,128)S(1)} %shard_map.117), channel_id=1, replica_groups={{0,16,64,80,128,144,192,208,256,272,320,336,384,400,448,464},{32,48,96,..., dimensions={0}, use_global_device_ids=true | all-gather | bytes 557056 | tf_op jit(solution)/shard_map/all_gather | solution.py:165
  277.1 2.0 shard_map.118
  279.1 15.1 %all_to_all.32.refs_0_ = f32[16,2,32,128]{3,2,1,0:T(8,128)S(1)} all-to-all(f32[16,2,32,128]{3,2,1,0:T(8,128)S(1)} %shard_map.118), channel_id=1, replica_groups=mesh['prow'=32,'pcol'=16] {'pcol'}, dimensions={0} | all-to-all | bytes 1048576 | tf_op jit(solution)/shard_map/all_to_all | solution.py:169
  294.3 21.5 %all_gather.23.refs_3_ = f32[32,32,128]{2,1,0:T(8,128)S(1)} all-gather(f32[2,32,128]{2,1,0:T(8,128)S(1)} %shard_map.119), channel_id=1, replica_groups={{0,16,64,80,128,144,192,208,256,272,320,336,384,400,448,464},{32,48,96,..., dimensions={0}, use_global_device_ids=true | all-gather | bytes 557056 | tf_op jit(solution)/shard_map/all_gather | solution.py:165
  315.8 2.0 shard_map.120
  317.8 14.9 %all_to_all.33.refs_0_ = f32[16,2,32,128]{3,2,1,0:T(8,128)S(1)} all-to-all(f32[16,2,32,128]{3,2,1,0:T(8,128)S(1)} %shard_map.120), channel_id=1, replica_groups=mesh['prow'=32,'pcol'=16] {'pcol'}, dimensions={0} | all-to-all | bytes 1048576 | tf_op jit(solution)/shard_map/all_to_all | solution.py:169
  333.0 1.9 collective-permute-start.8
  334.9 4.2 %collective-permute-done.8 = f32[4,32,128]{2,1,0:T(8,128)S(1)} collective-permute-done((f32[4,32,128]{2,1,0:T(8,128)S(1)}, f32[4,32,128]{2,1,0:T(8,128)S(1)}, u32[]{:S(2)}, u32[]{:S(2)}) %collective-permute-start.8) | collective-permute-done | bytes 65568 | tf_op jit(solution)/shard_map/ppermute | solution.py:158
  339.1 0.7 fusion
  (69 shorter events, 1.2 us)
Async XLA Ops:
  0.0 23.1 %copy-start = (f32[3,1,1,16,64,128]{5,4,3,2,1,0:T(8,128)S(1)}, f32[3,1,1,16,64,128]{5,4,3,2,1,0:T(8,128)}, u32[]{:S(2)}) copy-start(f32[3,1,1,16,64,128]{5,4,3,2,1,0:T(8,128)} %param.14) | copy-start | bytes 4718596
  0.0 1.1 copy-start.2
  1.1 0.9 copy-start.26
  2.0 18.5 %copy-start.3 = (f32[4,1,1,128,128]{4,3,2,1,0:T(8,128)S(1)}, f32[4,1,1,128,128]{4,3,2,1,0:T(8,128)}, u32[]{:S(2)}) copy-start(f32[4,1,1,128,128]{4,3,2,1,0:T(8,128)} %param.12) | copy-start | bytes 786436
  2.2 26.0 %collective-permute-start.1 = (f32[32,128]{1,0:T(8,128)S(1)}, f32[32,128]{1,0:T(8,128)S(1)}, u32[]{:S(2)}, u32[]{:S(2)}) collective-permute-start(f32[32,128]{1,0:T(8,128)S(1)} %get-tuple-element.16), channel_id=1, source_target_pairs={{0,32},{16,48},{32,0},{48,16},{64,96},{80,112},{96,64},{112,80},{1... | collective-permute-start | bytes 49160 | tf_op jit(solution)/shard_map/ppermute | solution.py:158
  13.5 64.8 %collective-permute-start = (s32[2,3,16,66]{3,2,1,0:T(8,128)S(1)}, s32[2,3,16,66]{3,2,1,0:T(8,128)S(1)}, u32[]{:S(2)}, u32[]{:S(2)}) collective-permute-start(s32[2,3,16,66]{3,2,1,0:T(8,128)S(1)} %get-tuple-element.14), channel_id=1, source_target_pairs={{0,32},{16,48},{32,0},{48,16},{64,96},{80,112},{96,64},{112,80},{1... | collective-permute-start | bytes 76040 | tf_op jit(solution)/shard_map/ppermute | solution.py:158
  16.5 62.4 %collective-permute-start.2 = (f32[1,16,64,128]{3,2,1,0:T(8,128)S(1)}, f32[1,16,64,128]{3,2,1,0:T(8,128)S(1)}, u32[]{:S(2)}, u32[]{:S(2)}) collective-permute-start(f32[1,16,64,128]{3,2,1,0:T(8,128)S(1)} %slice_bitcast_fusion.1), channel_id=1, source_target_pairs={{0,32},{16,48},{32,0},{48,16},{64,96},{80,112},{96,64},{112,80},{1... | collective-permute-start | bytes 1572872 | tf_op jit(solution)/shard_map/ppermute | solution.py:158
  21.2 78.2 %collective-permute-start.4 = (f32[3,128,128]{2,1,0:T(8,128)}, f32[3,128,128]{2,1,0:T(8,128)}, u32[]{:S(2)}, u32[]{:S(2)}) collective-permute-start(f32[3,128,128]{2,1,0:T(8,128)} %slice_bitcast_fusion.2), channel_id=1, source_target_pairs={{0,32},{16,48},{32,0},{48,16},{64,96},{80,112},{96,64},{112,80},{1... | collective-permute-start | bytes 589832 | tf_op jit(solution)/shard_map/ppermute | solution.py:158
  24.2 126.0 %collective-permute-start.5 = (f32[2,16,64,128]{3,2,1,0:T(8,128)}, f32[2,16,64,128]{3,2,1,0:T(8,128)}, u32[]{:S(2)}, u32[]{:S(2)}) collective-permute-start(f32[2,16,64,128]{3,2,1,0:T(8,128)} %slice_bitcast_fusion), channel_id=1, source_target_pairs={{0,32},{16,48},{32,0},{48,16},{64,96},{80,112},{96,64},{112,80},{1... | collective-permute-start | bytes 3145736 | tf_op jit(solution)/shard_map/ppermute | solution.py:158
  77.7 0.6 copy-start.14
  78.8 5.1 %copy-start.27 = (s32[192]{0:T(256)}, s32[192]{0:T(256)S(1)}, u32[]{:S(2)}) copy-start(s32[192]{0:T(256)S(1)} %add.17.refs_0_) | copy-start | bytes 2308
  78.9 5.1 %copy-start.30 = (s32[192]{0:T(256)}, s32[192]{0:T(256)S(1)}, u32[]{:S(2)}) copy-start(s32[192]{0:T(256)S(1)} %reshape_squeeze.4.refs_1_) | copy-start | bytes 2308
  79.0 0.8 copy-start.20
  79.8 1.0 copy-start.13
  80.8 1.0 copy-start.21
  81.9 13.9 %copy-start.1 = (f32[3,1,1,16,64,128]{5,4,3,2,1,0:T(8,128)S(1)}, f32[3,1,1,16,64,128]{5,4,3,2,1,0:T(8,128)}, u32[]{:S(2)}) copy-start(f32[3,1,1,16,64,128]{5,4,3,2,1,0:T(8,128)} %param.18) | copy-start | bytes 4718596
  83.9 0.8 copy-start.12
  84.7 19.2 %all-to-all-start = ((f32[16,2,32,128]{3,2,1,0:T(8,128)}), f32[16,2,32,128]{3,2,1,0:T(8,128)}, u32[]{:S(2)}, u32[]{:S(2)}) async-start(f32[16,2,32,128]{3,2,1,0:T(8,128)} %copy-done.12), calls=%async_computation | async-start | bytes 1048576 | tf_op jit(solution)/shard_map/all_to_all | solution.py:169
  92.7 6.0 %collective-permute-start.3 = (f32[3,32,128]{2,1,0:T(8,128)S(1)}, f32[3,32,128]{2,1,0:T(8,128)S(1)}, u32[]{:S(2)}, u32[]{:S(2)}) collective-permute-start(f32[3,32,128]{2,1,0:T(8,128)S(1)} %get-tuple-element.11), channel_id=1, source_target_pairs={{0,32},{16,48},{32,0},{48,16},{64,96},{80,112},{96,64},{112,80},{1... | collective-permute-start | bytes 147464 | tf_op jit(solution)/shard_map/ppermute | solution.py:158
  95.8 142.0 %collective-permute-start.7 = (f32[3,16,64,128]{3,2,1,0:T(8,128)S(1)}, f32[3,16,64,128]{3,2,1,0:T(8,128)}, u32[]{:S(2)}, u32[]{:S(2)}) collective-permute-start(f32[3,16,64,128]{3,2,1,0:T(8,128)S(1)} %bitcast.51), channel_id=1, source_target_pairs={{0,32},{16,48},{32,0},{48,16},{64,96},{80,112},{96,64},{112,80},{1... | collective-permute-start | bytes 4718600 | tf_op jit(solution)/shard_map/ppermute | solution.py:158
  98.7 0.6 copy-start.22
  103.9 46.3 %copy-start.28 = (s32[192]{0:T(256)S(1)}, s32[192]{0:T(256)}, u32[]{:S(2)}) copy-start(s32[192]{0:T(256)} %copy-done.27) | copy-start | bytes 2308
  103.9 0.8 copy-start.23
  104.7 45.5 %copy-start.31 = (s32[192]{0:T(256)S(1)}, s32[192]{0:T(256)}, u32[]{:S(2)}) copy-start(s32[192]{0:T(256)} %copy-done.30) | copy-start | bytes 2308
  105.9 44.3 %copy-start.16 = (f32[2,32,128]{2,1,0:T(8,128)}, f32[2,32,128]{2,1,0:T(8,128)S(1)}, u32[]{:S(2)}) copy-start(f32[2,32,128]{2,1,0:T(8,128)S(1)} %shard_map.111.refs_1_.refs_2_) | copy-start | bytes 98308
  150.2 21.6 %copy-start.24 = (f32[3,32,128]{2,1,0:T(8,128)S(1)}, f32[3,32,128]{2,1,0:T(8,128)}, u32[]{:S(2)}) copy-start(f32[3,32,128]{2,1,0:T(8,128)} %copy-done.22) | copy-start | bytes 147460
  190.4 0.6 copy-start.18
  193.6 0.8 copy-start.11
  194.4 15.9 %all-to-all-start.2 = ((f32[16,2,32,128]{3,2,1,0:T(8,128)}), f32[16,2,32,128]{3,2,1,0:T(8,128)S(1)}, u32[]{:S(2)}, u32[]{:S(2)}) async-start(f32[16,2,32,128]{3,2,1,0:T(8,128)} %copy-done.11), calls=%async_computation.2 | async-start | bytes 1048576 | tf_op jit(solution)/shard_map/all_to_all | solution.py:169
  198.0 10.8 %collective-permute-start.6 = (f32[4,128,128]{2,1,0:T(8,128)}, f32[4,128,128]{2,1,0:T(8,128)S(1)}, u32[]{:S(2)}, u32[]{:S(2)}) collective-permute-start(f32[4,128,128]{2,1,0:T(8,128)} %bitcast.60), channel_id=1, source_target_pairs={{0,32},{16,48},{32,0},{48,16},{64,96},{80,112},{96,64},{112,80},{1... | collective-permute-start | bytes 786440 | tf_op jit(solution)/shard_map/ppermute | solution.py:158
  208.7 0.7 copy-start.6
  210.3 0.8 copy-start.9
  211.1 0.9 copy-start.4
  212.0 0.9 copy-start.7
  213.0 1.0 copy-start.10
  214.0 0.8 copy-start.25
  237.9 21.3 %copy-start.5 = (f32[4,1,1,128,128]{4,3,2,1,0:T(8,128)S(1)}, f32[4,1,1,128,128]{4,3,2,1,0:T(8,128)}, u32[]{:S(2)}) copy-start(f32[4,1,1,128,128]{4,3,2,1,0:T(8,128)} %param.13) | copy-start | bytes 786436
  237.9 21.3 %copy-start.8 = (f32[4,128,128]{2,1,0:T(8,128)S(1)}, f32[4,128,128]{2,1,0:T(8,128)}, u32[]{:S(2)}) copy-start(f32[4,128,128]{2,1,0:T(8,128)} %copy-done.6) | copy-start | bytes 786436
  237.9 21.3 %copy-start.19 = (f32[2,32,128]{2,1,0:T(8,128)S(1)}, f32[2,32,128]{2,1,0:T(8,128)}, u32[]{:S(2)}) copy-start(f32[2,32,128]{2,1,0:T(8,128)} %copy-done.18) | copy-start | bytes 98308
  237.9 0.7 copy-start.29
  238.6 0.6 copy-start.32
  277.1 17.1 %copy-start.17 = (f32[2,32,128]{2,1,0:T(8,128)S(1)}, f32[2,32,128]{2,1,0:T(8,128)}, u32[]{:S(2)}) copy-start(f32[2,32,128]{2,1,0:T(8,128)} %copy-done.16) | copy-start | bytes 98308
  315.8 16.9 %copy-start.15 = (f32[2,32,128]{2,1,0:T(8,128)S(1)}, f32[2,32,128]{2,1,0:T(8,128)}, u32[]{:S(2)}) copy-start(f32[2,32,128]{2,1,0:T(8,128)} %copy-done.14) | copy-start | bytes 98308
  333.0 6.2 %collective-permute-start.8 = (f32[4,32,128]{2,1,0:T(8,128)S(1)}, f32[4,32,128]{2,1,0:T(8,128)S(1)}, u32[]{:S(2)}, u32[]{:S(2)}) collective-permute-start(f32[4,32,128]{2,1,0:T(8,128)S(1)} %get-tuple-element.10), channel_id=1, source_target_pairs={{0,32},{16,48},{32,0},{48,16},{64,96},{80,112},{96,64},{112,80},{1... | collective-permute-start | bytes 196616 | tf_op jit(solution)/shard_map/ppermute | solution.py:158

commit v2 on v1

v2 whole, which is shorter than its diff:
```python
import jax
import jax.numpy as jnp
from jax import lax
from jax.experimental import pallas as pl
from jax.experimental.pallas import tpu as pltpu
from jax.sharding import PartitionSpec as P

F32 = jnp.float32
BF16 = jnp.bfloat16
SMALL_VMEM = 12 * 1024 * 1024
LARGE_VMEM = 60 * 1024 * 1024
STEP_ROWS = 32


def dot_nt(a, b):
    return lax.dot_general(a, b, (((1,), (1,)), ((), ())), preferred_element_type=F32)


def dot_nn(a, b):
    return lax.dot_general(a, b, (((1,), (0,)), ((), ())), preferred_element_type=F32)


def split(x):
    high = x.astype(BF16)
    low = (x - high.astype(F32)).astype(BF16)
    return jnp.concatenate([high, low], axis=0)


def fold(x):
    half = x.shape[0] // 2
    return x[:half] + x[half:]


def apply_inverse(vectors, inverse):
    size = inverse.shape[0]
    out = fold(dot_nt(split(vectors), split(inverse)))
    return out[:, :size] + out[:, size:]


def structure_matrix(rows):
    positions = lax.broadcasted_iota(jnp.int32, (128, rows.shape[1]), 0).astype(rows.dtype)
    return jnp.where(positions == rows, 1.0, 0.0).astype(BF16)


def pick(array, *at):
    tail = array.shape[len(at) :]
    return pl.BlockSpec((None,) * len(at) + tail, lambda i: tuple(at) + (0,) * len(tail))


def rows_of(array, first, count, memory_space=None):
    assert first % count == 0
    return pl.BlockSpec((2, count, array.shape[2]), lambda i: (0, first // count, 0), memory_space=memory_space)


def scalars():
    return pl.BlockSpec(memory_space=pltpu.SMEM)


def call(kernel, outs, in_specs, operands, vmem=SMALL_VMEM, flops=1 << 24, scratch=(), grid=(1,)):
    return pl.pallas_call(
        kernel,
        grid=grid,
        out_shape=outs,
        in_specs=in_specs,
        out_specs=[pick(o) for o in outs],
        scratch_shapes=scratch,
        compiler_params=pltpu.CompilerParams(vmem_limit_bytes=vmem),
        cost_estimate=pl.CostEstimate(flops=flops, bytes_accessed=1 << 20, transcendentals=0),
    )(*operands)


def own_products_kernel(transposed, level, parity_ref, source_ref, target_ref, rows_ref, near_ref, far_ref, tiles_ref, out_ref, parts_ref):
    tiles = tiles_ref.shape[0]
    rows = rows_ref[...]
    rows = jnp.concatenate([rows, rows], axis=1)
    for first in range(0, tiles, 4):
        held = []
        for k in range(first, first + 4):
            source = source_ref[level, 0, 0, k]
            at = 2 * (source >> 2) + (source & 1)
            is_near = ((source >> 1) & 1) == parity_ref[0]
            block = split(jnp.where(is_near, near_ref[at], far_ref[at]))
            tile = split(tiles_ref[k])
            places = structure_matrix(rows[k : k + 1, :])
            if transposed:
                held.append((k, fold(dot_nt(block, tile)), places))
            else:
                held.append((k, dot_nn(block, places).astype(BF16), tile))
        for k, left, right in held:
            if transposed:
                parts_ref[k] = fold(dot_nt(split(left), right))
            else:
                parts_ref[k] = fold(dot_nn(left, right))
    out_ref[...] = jnp.zeros_like(out_ref)
    for k in range(tiles):
        out_ref[target_ref[level, 0, 0, k]] += parts_ref[k]


def own_products(transposed, level, parity, source, target, rows, near, far, tiles):
    count, (nrhs, width) = tiles.shape[3], near.shape[1:]
    outs = [jax.ShapeDtypeStruct((16, nrhs, width), F32)]
    in_specs = [scalars()] * 3 + [pick(rows, level, 0, 0), pick(near), pick(far), pick(tiles, level, 0, 0)]
    operands = (parity, source, target, rows, near, far, tiles)
    kernel = lambda *refs: own_products_kernel(transposed, level, *refs)
    return call(kernel, outs, in_specs, operands, flops=1 << 28, scratch=[pltpu.VMEM((count, nrhs, width), F32)])[0]


def products_kernel(transposed, tiles, height, at_ref, ints_ref, blocks_ref, tiles_ref, out_ref, parts_ref):
    first_lane = 0 if transposed else height
    rows = []
    for row in range(2):
        once = ints_ref[row, :tiles, first_lane : first_lane + height]
        rows.append(jnp.concatenate([once, once], axis=1))

    def scalar(row, kind, k):
        return at_ref[row, tiles + kind, first_lane + k].astype(jnp.int32)

    for first in range(0, 2 * tiles, 8):
        group = range(first, first + 8)
        held = []
        for t in group:
            row, k = divmod(t, tiles)
            at = scalar(row, 0, k)
            block = split(blocks_ref[(at & ~3) + 2 * (at & 1) + ((at >> 1) & 1)])
            tile = split(tiles_ref[row, k * height : (k + 1) * height, :])
            places = structure_matrix(rows[row][k : k + 1, :])
            if transposed:
                held.append((fold(dot_nt(block, tile)), places))
            else:
                held.append((dot_nn(block, places).astype(BF16), tile))
        for t, (left, right) in zip(group, held):
            if transposed:
                parts_ref[t] = fold(dot_nt(split(left), right))
            else:
                parts_ref[t] = fold(dot_nn(left, right))
    out_ref[...] = jnp.zeros_like(out_ref)
    for t in range(2 * tiles):
        row, k = divmod(t, tiles)
        out_ref[scalar(row, 1, k), row] += parts_ref[t]


def products(transposed, structure, structure_at, blocks, bundle, tiles, height):
    half, width = blocks.shape[1:]
    outs = [jax.ShapeDtypeStruct((16, 2, half, width), F32)]
    in_specs = [
        rows_of(structure, structure_at, STEP_ROWS, pltpu.SMEM),
        rows_of(structure, structure_at, STEP_ROWS),
        pick(blocks),
        rows_of(bundle, 0, tiles * height),
    ]
    scratch = [pltpu.VMEM((2 * tiles, half, width), F32)]
    kernel = lambda *refs: products_kernel(transposed, tiles, height, *refs)
    return call(kernel, outs, in_specs, (structure, structure, blocks, bundle), flops=1 << 28, scratch=scratch)[0]


def summed(parts_ref):
    total = parts_ref[0]
    for k in range(1, parts_ref.shape[0]):
        total = total + parts_ref[k]
    return total


def solve_kernel(mine, inverses, *refs):
    if mine:
        parity_ref, refs = refs[0], refs[1:]
    parts_ref, start_ref, inverse_refs, rest = refs[0], refs[1], refs[2 : 2 + inverses], refs[2 + inverses :]
    total = parts_ref[0]
    for k in range(1, parts_ref.shape[0]):
        total = total + parts_ref[k]
    if total.ndim == 2:
        rest[0][...] = apply_inverse(start_ref[...] - total, inverse_refs[0][...])
        return
    half = total.shape[1]
    stacked = len(rest[-1].shape) == 4
    for row in range(2):
        if mine:
            start = start_ref[row, pl.ds(pl.multiple_of(parity_ref[0] * half, half), half), :]
        else:
            start = start_ref[row]
        value = start - total[row]
        for k, inverse_ref in enumerate(inverse_refs):
            value = apply_inverse(value, inverse_ref[row])
            if stacked:
                rest[-1][0, row] = value
            else:
                rest[k][row] = value
    if stacked:
        for k, ref in enumerate(rest[:-1]):
            rest[-1][k + 1] = ref[...]


def first_forward(parts, rhs, inverse, level):
    outs = [jax.ShapeDtypeStruct(parts.shape[1:], F32)]
    in_specs = [pick(parts), pick(rhs, level, 0, 0), pick(inverse, level, 0, 0)]
    return call(lambda *refs: solve_kernel(False, 1, *refs), outs, in_specs, (parts, rhs, inverse))[0]


def pair_solve(parity, parts, start, inverses, higher=()):
    _, _, half, width = parts.shape
    shape = jax.ShapeDtypeStruct(parts.shape[1:], F32)
    whole = isinstance(start, tuple)
    in_specs, operands = ([scalars()], [parity]) if whole else ([], [])
    in_specs += [pick(parts), rows_of(*start, 2 * half) if whole else pick(start)]
    operands += [parts, start[0] if whole else start]
    in_specs += [rows_of(*inverse, width) for inverse in inverses] + [pick(h) for h in higher]
    operands += [inverse[0] for inverse in inverses] + list(higher)
    outs = [shape] * len(inverses)
    if higher:
        outs = [jax.ShapeDtypeStruct((len(higher) + 1,) + shape.shape, F32)]
    return call(lambda *refs: solve_kernel(whole, len(inverses), *refs), outs, in_specs, operands)


def first_kernel(rhs_ref, inv_ref, *rest):
    ints_refs, (out_ref, structure_ref) = rest[:6], rest[6:]
    out_ref[...] = apply_inverse(rhs_ref[...], inv_ref[...])
    structure_ref[...] = jnp.zeros_like(structure_ref)
    for factor in range(2):
        rows_ref, source_ref, target_ref = ints_refs[3 * factor : 3 * factor + 3]
        steps, _, _, tiles, height = rows_ref.shape
        lanes = factor * height
        for k in range(steps):
            at = k * STEP_ROWS
            structure_ref[at : at + tiles, lanes : lanes + height] = rows_ref[k, 0, 0].astype(F32)
            structure_ref[at + tiles : at + tiles + 1, lanes : lanes + tiles] = source_ref[k, 0].astype(F32)
            structure_ref[at + tiles + 1 : at + tiles + 2, lanes : lanes + tiles] = target_ref[k, 0].astype(F32)


def first_solve(rhs, inverse, *ints):
    nrhs, width = rhs.shape[3:]
    steps = ints[0].shape[0]
    outs = [jax.ShapeDtypeStruct((rows, width), F32) for rows in (nrhs, steps * STEP_ROWS)]
    in_specs = [pick(rhs, 0, 0, 0), pick(inverse, 0, 0, 0)] + [pick(a) for a in ints]
    return call(first_kernel, outs, in_specs, (rhs, inverse, *ints), vmem=LARGE_VMEM)


def bundles_kernel(plans, *refs):
    sems = refs[-1]
    outs = refs[-1 - len(plans) : -1]
    copies = []
    for plan, out_ref in zip(plans, outs):
        first = 0
        for operand, level, rows in plan:
            src = refs[operand] if level is None else refs[operand].at[level]
            copies.append(pltpu.make_async_copy(src, out_ref.at[pl.ds(first, rows)], sems.at[len(copies)]))
            copies[-1].start()
            first += rows
    for copy in copies:
        copy.wait()


def build_bundles(arrays, held):
    plans = [[(at, level, arrays[at].shape[-2]) for at, level in items] for items in held]
    width = arrays[0].shape[-1]
    outs = [jax.ShapeDtypeStruct((sum(rows for _, _, rows in plan), width), F32) for plan in plans]
    scratch = [pltpu.SemaphoreType.DMA((sum(len(plan) for plan in plans),))]
    in_specs = [pl.BlockSpec(memory_space=pl.ANY)] * len(arrays)
    return call(lambda *refs: bundles_kernel(plans, *refs), outs, in_specs, arrays, vmem=LARGE_VMEM, scratch=scratch)


def last_kernel(parity_ref, both_ref, out_ref):
    parity = parity_ref[0]
    half = both_ref.shape[3]
    for z in range(2):
        for k in range(both_ref.shape[1]):
            out_ref[k, 0, 0, z * half : (z + 1) * half, :] = both_ref[z, k, parity]


def last_step(parity, both):
    _, levels, _, half, width = both.shape
    outs = [jax.ShapeDtypeStruct((levels, 1, 1, 2 * half, width), F32)]
    return call(last_kernel, outs, [scalars(), pick(both)], (parity, both))[0]


def body(rhs, l_inverse, u_inverse, l_tiles, l_source, l_target, l_rows, u_tiles, u_source, u_target, u_cols):
    ints = (l_rows, l_source, l_target, u_cols, u_source, u_target)
    levels, nrhs, width = rhs.shape[0], rhs.shape[3], rhs.shape[4]
    half = nrhs // 2
    tiles, height = l_tiles.shape[3:5]
    prow = lax.axis_size("prow")
    at = (lax.axis_index("prow") >> 1) & 1
    parity = at.reshape(1).astype(jnp.int32)
    pairs = [[4 * i + c, 4 * i + 2 + c] for i in range(prow // 4) for c in range(2)]
    groups = [[4 * i + 2 * a + c for i in range(prow // 4) for c in range(2)] for a in range(2)]
    onward = [(r, (r + 2 if r % 2 == 0 else r - 2) % prow) for r in range(prow)]

    def both(array):
        return lax.all_gather(array, "prow", axis=0, tiled=False, axis_index_groups=pairs)

    def gather(value):
        return lax.all_gather(value, "prow", axis=0, tiled=True, axis_index_groups=groups)

    def exchange(parts):
        return lax.all_to_all(parts, "pcol", 0, 0, tiled=True)

    def after(array, earlier):
        return lax.optimization_barrier((array, earlier))

    first, structure = first_solve(rhs, l_inverse, *ints)
    near = gather(first[None])
    raw = (l_tiles, u_tiles, l_inverse, u_inverse, rhs)
    raw = [a.reshape(a.shape[0], -1, width) for a in raw] + [structure, first]
    near, *raw = lax.optimization_barrier((near, *raw))
    far = lax.ppermute(near, "prow", onward)
    held = [
        [(0, 1), (2, 2), (4, 2), (5, None)],
        [(0, 2), (2, 3), (3, 3), (4, 3)],
        [(1, 2), (3, 2)],
        [(1, 1), (3, 1)],
        [(1, 0), (3, 0), (6, None)],
    ]
    bundles = list(build_bundles(raw, held))
    parts = own_products(True, 0, parity, l_source, l_target, l_rows, near, far, l_tiles)
    in_tiles = tiles * height
    shared = [both(bundles[0])]
    second = first_forward(exchange(parts), rhs, l_inverse, 1)
    bundles[1], second = after(bundles[1], second)
    shared.append(both(bundles[1]))
    value = lax.dynamic_slice(both(second), (0, at * half, 0), (2, half, width))
    forward = [None, value]
    result = []
    for step, level in enumerate([2, 3, 2, 1, 0]):
        is_forward = step < 2
        mine = shared[step]
        if step:
            mine, value = after(mine, value)
        blocks = gather(value).reshape(prow, half, width)
        if step + 2 < len(bundles):
            later, blocks = after(bundles[step + 2], blocks)
            shared.append(both(later))
        structure_at = in_tiles + width + nrhs + (level - 1 if is_forward else level) * STEP_ROWS
        parts = products(is_forward, shared[0], structure_at, blocks, mine, tiles, height)
        got = exchange(parts)
        if step == 0:
            (value,) = pair_solve(parity, got, (mine, in_tiles + width), [(mine, in_tiles)])
            forward.append(value)
            continue
        if step == 1:
            inverses = [(mine, in_tiles), (mine, in_tiles + width)]
            _, value = pair_solve(parity, got, (mine, in_tiles + 2 * width), inverses)
        elif level > 0:
            (value,) = pair_solve(parity, got, forward[level], [(mine, in_tiles)])
        else:
            (value,) = pair_solve(parity, got, (mine, in_tiles + width), [(mine, in_tiles)], result[::-1])
        result.append(value)
    return last_step(parity, both(value))


def solution(mesh):
    spec = lambda tail: P(None, "prow", "pcol", *([None] * tail))
    in_specs = tuple(spec(n) for n in (2, 2, 2, 3, 1, 1, 2, 3, 1, 1, 2))
    return jax.shard_map(body, mesh=mesh, in_specs=in_specs, out_specs=spec(2), check_vma=False)
```

time: 341 us -> 289 us (0.85)
  starting transfers between devices: 41.2 us -> 5.79 us
  blocking collectives: 239 us -> 219 us
  local copies, waits for them, and re-layouts: 22.8 us -> 7.33 us
  between operations: 0.34 us -> 13.3 us
  waiting for transfers between devices: 16.8 us -> 21.5 us
    all_gather x6, blocking collectives: 172 us -> 127 us  [gather(): lax.all_gather(value, 'prow', axis=0, tiled=True, axis_index_groups=groups)]
    ppermute x9 -> x1, starting transfers between devices: 30.6 us -> 1.92 us  [body(): far = lax.ppermute(near, 'prow', onward)]
    all_to_all x4 -> x5, blocking collectives: 67.1 us -> 81.6 us  [exchange(): return lax.all_to_all(parts, 'pcol', 0, 0, tiled=True)]
    all_gather x0 -> x2, blocking collectives: none -> 10.2 us  [both(): lax.all_gather(array, 'prow', axis=0, tiled=False, axis_index_groups=pairs)]
    unnamed x66 -> x32, local copies, waits for them, and re-layouts: 15.7 us -> 7.33 us
    all_to_all x2 -> x1, starting transfers between devices: 10.7 us -> 3.7 us  [exchange(): return lax.all_to_all(parts, 'pcol', 0, 0, tiled=True)]
    all_to_all x2 -> x1, waiting for transfers between devices: 5.38 us -> 11.7 us  [exchange(): return lax.all_to_all(parts, 'pcol', 0, 0, tiled=True)]
    slice x4 -> x0, local copies, waits for them, and re-layouts: 3.79 us -> none  [the longest x1 1.11 us: body(): l_rest = swap(l_tiles[1:])]
  transfers between devices with their start and end apart: 11 -> 7, of which waited for: 5 -> 2; matrix products, arithmetic and copies ran while one was open for 2% -> 0% of each run, Pallas kernels for 3% -> 4%
where the time goes in v2:
time: 289 us; the launch traced here: 288 us
  blocking collectives  219 us (76%)
  waiting for transfers between devices  21.5 us (7%)
  Pallas kernels  20.5 us (7%)
  between operations  13.3 us (5%)
  local copies, waits for them, and re-layouts  7.33 us (3%)
  starting transfers between devices  5.79 us (2%)
    all_gather x6, blocking collectives, gather(): lax.all_gather(value, 'prow', axis=0, tiled=True, axis_index_groups=groups)  127 us
    all_to_all x5, blocking collectives, exchange(): return lax.all_to_all(parts, 'pcol', 0, 0, tiled=True)  81.6 us
    pallas_call x15, Pallas kernels, call(): pl.pallas_call(kernel, grid=grid, out_shape=outs, in_specs=in_specs, out_...  20.5 us
    all_to_all x1, waiting for transfers between devices, exchange(): return lax.all_to_all(parts, 'pcol', 0, 0, tiled=True)  11.7 us
    all_gather x2, blocking collectives, both(): lax.all_gather(array, 'prow', axis=0, tiled=False, axis_index_groups=pairs)  10.2 us
    ppermute x1, waiting for transfers between devices, body(): far = lax.ppermute(near, 'prow', onward)  9.14 us
    unnamed x32, local copies, waits for them, and re-layouts  7.33 us
  transfers between devices with their start and end apart: 7, of which 2 were waited for; matrix products, arithmetic and copies ran while one was open for 0% of the time, Pallas kernels for 4%

profile of v2, /device:TPU:32, one launch (start us, length us, event | category | flops | bytes accessed | tf_op | source)
XLA Modules:
  0.0 287.8 jit_solution(6458817049135919933)
XLA Ops:
  6.5 0.0 all-gather.14.cloned.1.call-start
  6.5 1.6 shard_map.109
  8.2 26.6 %all-gather = f32[1024,128]{1,0:T(8,128)S(1)} all-gather(f32[64,128]{1,0:T(8,128)} %get-tuple-element.45.refs_6_), channel_id=2, replica_groups={{0,16,64,80,128,144,192,208,256,272,320,336,384,400,448,464},{32,48,96,..., dimensions={0}, use_global_device_ids=true | all-gather | bytes 557056 | tf_op jit(solution)/shard_map/all_gather | solution.py:290
  34.8 3.7 %shard_map.110 = (f32[1312,128]{1,0:T(8,128)}, f32[1344,128]{1,0:T(8,128)}, f32[1152,128]{1,0:T(8,128)}, f32[1152,128]{1,0:T(8,128)}, f32[1216,128]{1,0:T(8,128)}) custom-call(f32[3,1024,128]{2,1,0:T(8,128)} %bitcast.34, f32[3,1024,128]{2,1,0:T(8,128)} %bitcast.44, f32[4,128,128]{2,1,0:T(8,128)} %bitcast.39, f32[4,128,128]{2,1,0:T(8,128)} %bitcast.45, ...), custom_call_target="tpu_custom_call" | custom-call | flops 16777216 | bytes 1048576 | tf_op jit(solution)/shard_map/pallas_call | solution.py:60
  38.6 0.0 all-gather.14.cloned.1.call-update
  38.6 0.0 all-gather.18.cloned.1.call-start
  38.7 1.9 collective-permute-start
  40.6 9.1 %collective-permute-done.refs_5_ = f32[16,64,128]{2,1,0:T(8,128)S(1)} collective-permute-done((f32[16,64,128]{2,1,0:T(8,128)S(1)}, f32[16,64,128]{2,1,0:T(8,128)S(1)}, u32[]{:S(2)}, u32[]{:S(2)}) %collective-permute-start) | collective-permute-done | bytes 524320 | tf_op jit(solution)/shard_map/ppermute | solution.py:303
  49.7 0.0 copy-done.6
  49.7 0.0 copy-done.13
  49.7 0.0 copy-done.14
  49.7 0.0 copy-done.15
  49.8 0.0 copy-start.10
  49.8 0.0 copy-start.12
  49.8 1.6 shard_map.111
  51.4 18.0 %all_to_all.30.refs_0_ = f32[16,64,128]{2,1,0:T(8,128)S(1)} all-to-all(f32[16,64,128]{2,1,0:T(8,128)S(1)} %shard_map.111), channel_id=1, replica_groups=mesh['prow'=32,'pcol'=16] {'pcol'}, dimensions={0} | all-to-all | bytes 1048576 | tf_op jit(solution)/shard_map/all_to_all | solution.py:293
  69.4 0.0 copy-done.10
  69.4 0.0 copy-done.12
  69.4 0.2 shard_map.112
  69.6 0.0 all-gather.18.cloned.1.call-update
  69.6 0.0 all-gather.16.cloned.1.call-start
  69.6 4.6 %all-gather.2 = f32[128,128]{1,0:T(8,128)S(1)} all-gather(f32[64,128]{1,0:T(8,128)S(1)} %shard_map.112), channel_id=4, replica_groups={{0,32},{16,48},{64,96},{80,112},{128,160},{144,176},{192,224},{208,240}..., dimensions={0}, use_global_device_ids=true | all-gather | bytes 98304 | tf_op jit(solution)/shard_map/all_gather | solution.py:287
  74.2 20.3 %all_gather.65.refs_2_ = f32[32,32,128]{2,1,0:T(8,128)S(1)} all-gather(f32[2,32,128]{2,1,0:T(8,128)S(1)} %constant_dynamic-slice_fusion.refs_1_), channel_id=1, replica_groups={{0,16,64,80,128,144,192,208,256,272,320,336,384,400,448,464},{32,48,96,..., dimensions={0}, use_global_device_ids=true | all-gather | bytes 557056 | tf_op jit(solution)/shard_map/all_gather | solution.py:290
  94.6 0.0 all-gather.16.cloned.1.call-update
  94.6 0.0 all-gather.22.cloned.1.call-start
  94.6 0.0 all-gather.14.cloned.1.call-done
  94.7 0.0 copy-start
  94.7 1.3 copy-done
  96.0 2.5 shard_map.113
  98.5 15.6 %all_to_all.31.refs_1_ = f32[16,2,32,128]{3,2,1,0:T(8,128)S(1)} all-to-all(f32[16,2,32,128]{3,2,1,0:T(8,128)S(1)} %shard_map.113), channel_id=1, replica_groups=mesh['prow'=32,'pcol'=16] {'pcol'}, dimensions={0} | all-to-all | bytes 1048576 | tf_op jit(solution)/shard_map/all_to_all | solution.py:293
  114.1 0.0 copy-done.1
  114.1 0.2 shard_map.114.refs_1_
  114.3 0.0 all-gather.18.cloned.1.call-done
  114.3 19.2 %all_gather.70.refs_2_ = f32[32,32,128]{2,1,0:T(8,128)S(1)} all-gather(f32[2,32,128]{2,1,0:T(8,128)S(1)} %shard_map.114.refs_1_), channel_id=1, replica_groups={{0,16,64,80,128,144,192,208,256,272,320,336,384,400,448,464},{32,48,96,..., dimensions={0}, use_global_device_ids=true | all-gather | bytes 557056 | tf_op jit(solution)/shard_map/all_gather | solution.py:290
  133.5 0.0 all-gather.22.cloned.1.call-update
  133.5 0.0 copy-start.2
  133.5 1.3 copy-done.2
  134.9 2.5 shard_map.115
  137.4 18.1 %all_to_all.32.refs_1_ = f32[16,2,32,128]{3,2,1,0:T(8,128)S(1)} all-to-all(f32[16,2,32,128]{3,2,1,0:T(8,128)S(1)} %shard_map.115), channel_id=1, replica_groups=mesh['prow'=32,'pcol'=16] {'pcol'}, dimensions={0} | all-to-all | bytes 1048576 | tf_op jit(solution)/shard_map/all_to_all | solution.py:293
  155.5 0.8 shard_map.116
  156.3 21.2 %all_gather.71.refs_2_ = f32[32,32,128]{2,1,0:T(8,128)S(1)} all-gather(f32[2,32,128]{2,1,0:T(8,128)S(1)} %get-tuple-element.60.refs_6_), channel_id=1, replica_groups={{0,16,64,80,128,144,192,208,256,272,320,336,384,400,448,464},{32,48,96,..., dimensions={0}, use_global_device_ids=true | all-gather | bytes 557056 | tf_op jit(solution)/shard_map/all_gather | solution.py:290
  177.5 1.3 copy-done.7
  178.8 2.1 shard_map.117
  180.9 0.0 copy-start.11
  180.9 0.8 copy-done.11
  181.7 3.7 %all-to-all-start.3 = ((f32[16,2,32,128]{3,2,1,0:T(8,128)}), f32[16,2,32,128]{3,2,1,0:T(8,128)S(1)}, u32[]{:S(2)}, u32[]{:S(2)}) async-start(f32[16,2,32,128]{3,2,1,0:T(8,128)} %copy-done.11), calls=%async_computation.3 | async-start | bytes 1048576 | tf_op jit(solution)/shard_map/all_to_all | solution.py:293
  185.4 0.0 all-gather.20.cloned.1.call-start
  185.5 0.5 all-gather.20.cloned.1.call-update
  186.0 11.7 %all-to-all-done.3.refs_0_ = f32[16,2,32,128]{3,2,1,0:T(8,128)S(1)} async-done(((f32[16,2,32,128]{3,2,1,0:T(8,128)}), f32[16,2,32,128]{3,2,1,0:T(8,128)S(1)}, u32[]{:S(2)}, u32[]{:S(2)}) %all-to-all-start.3) | async-done | bytes 524320 | tf_op jit(solution)/shard_map/all_to_all | solution.py:293
  197.7 0.2 shard_map.118.refs_5_
  197.9 0.0 all-gather.22.cloned.1.call-done
  197.9 20.0 %all_gather.76.refs_2_ = f32[32,32,128]{2,1,0:T(8,128)S(1)} all-gather(f32[2,32,128]{2,1,0:T(8,128)S(1)} %shard_map.118.refs_5_), channel_id=1, replica_groups={{0,16,64,80,128,144,192,208,256,272,320,336,384,400,448,464},{32,48,96,..., dimensions={0}, use_global_device_ids=true | all-gather | bytes 557056 | tf_op jit(solution)/shard_map/all_gather | solution.py:290
  217.9 1.3 copy-done.9
  219.1 2.1 shard_map.119
  221.2 14.9 %all_to_all.33.refs_0_ = f32[16,2,32,128]{3,2,1,0:T(8,128)S(1)} all-to-all(f32[16,2,32,128]{3,2,1,0:T(8,128)S(1)} %shard_map.119), channel_id=1, replica_groups=mesh['prow'=32,'pcol'=16] {'pcol'}, dimensions={0} | all-to-all | bytes 1048576 | tf_op jit(solution)/shard_map/all_to_all | solution.py:293
  236.2 0.2 shard_map.120.refs_4_
  236.3 0.0 all-gather.20.cloned.1.call-done
  236.3 20.1 %all_gather.77.refs_2_ = f32[32,32,128]{2,1,0:T(8,128)S(1)} all-gather(f32[2,32,128]{2,1,0:T(8,128)S(1)} %shard_map.120.refs_4_), channel_id=1, replica_groups={{0,16,64,80,128,144,192,208,256,272,320,336,384,400,448,464},{32,48,96,..., dimensions={0}, use_global_device_ids=true | all-gather | bytes 557056 | tf_op jit(solution)/shard_map/all_gather | solution.py:290
  256.5 1.3 copy-done.4
  257.8 2.1 shard_map.121
  259.9 14.9 %all_to_all.34.refs_1_ = f32[16,2,32,128]{3,2,1,0:T(8,128)S(1)} all-to-all(f32[16,2,32,128]{3,2,1,0:T(8,128)S(1)} %shard_map.121), channel_id=1, replica_groups=mesh['prow'=32,'pcol'=16] {'pcol'}, dimensions={0} | all-to-all | bytes 1048576 | tf_op jit(solution)/shard_map/all_to_all | solution.py:293
  274.8 0.2 shard_map.122
  275.0 5.6 %all-gather.7 = f32[8,2,32,128]{3,2,1,0:T(8,128)S(1)} all-gather(f32[4,2,32,128]{3,2,1,0:T(8,128)S(1)} %shard_map.122), channel_id=9, replica_groups={{0,32},{16,48},{64,96},{80,112},{128,160},{144,176},{192,224},{208,240}..., dimensions={0}, use_global_device_ids=true | all-gather | bytes 393216 | tf_op jit(solution)/shard_map/all_gather | solution.py:287
  280.6 0.7 shard_map.123
  (16 shorter events, 0.0 us)
Async XLA Ops:
  6.5 88.1 %all-gather.14.cloned.1.call-start = ((), (), s32[]{:S(2)}) async-start(), calls=%async_computation.6 | async-start | bytes 2015232 | tf_op jit(solution)/shard_map/all_gather | solution.py:287
  34.8 14.9 %copy-start.6 = (f32[3,1,1,16,64,128]{5,4,3,2,1,0:T(8,128)S(1)}, f32[3,1,1,16,64,128]{5,4,3,2,1,0:T(8,128)}, u32[]{:S(2)}) copy-start(f32[3,1,1,16,64,128]{5,4,3,2,1,0:T(8,128)} %refs_6_.1) | copy-start | bytes 4718596
  34.8 14.9 %copy-start.13 = (s32[3,1,1,16,64]{4,3,2,1,0:T(8,128)S(1)}, s32[3,1,1,16,64]{4,3,2,1,0:T(8,128)}, u32[]{:S(2)}) copy-start(s32[3,1,1,16,64]{4,3,2,1,0:T(8,128)} %refs_3_.1) | copy-start | bytes 36868
  34.8 14.9 %copy-start.14 = (s32[3,1,1,16]{3,2,1,0:T(1,128)S(1)}, s32[3,1,1,16]{3,2,1,0:T(1,128)}, u32[]{:S(2)}) copy-start(s32[3,1,1,16]{3,2,1,0:T(1,128)} %refs_1_.2) | copy-start | bytes 580
  34.8 14.9 %copy-start.15 = (s32[3,1,1,16]{3,2,1,0:T(1,128)S(1)}, s32[3,1,1,16]{3,2,1,0:T(1,128)}, u32[]{:S(2)}) copy-start(s32[3,1,1,16]{3,2,1,0:T(1,128)} %refs_2_.2) | copy-start | bytes 580
  38.6 75.7 %all-gather.18.cloned.1.call-start = ((), (), s32[]{:S(2)}) async-start(), calls=%async_computation.8 | async-start | bytes 2064384 | tf_op jit(solution)/shard_map/all_gather | solution.py:287
  38.7 11.1 %collective-permute-start = (f32[16,64,128]{2,1,0:T(8,128)S(1)}, f32[16,64,128]{2,1,0:T(8,128)S(1)}, u32[]{:S(2)}, u32[]{:S(2)}) collective-permute-start(f32[16,64,128]{2,1,0:T(8,128)S(1)} %bitcast.40), channel_id=1, source_target_pairs={{0,32},{16,496},{32,64},{48,16},{64,96},{80,48},{96,128},{112,80},... | collective-permute-start | bytes 1572872 | tf_op jit(solution)/shard_map/ppermute | solution.py:303
  49.8 19.6 %copy-start.10 = (f32[4,1,1,128,128]{4,3,2,1,0:T(8,128)S(1)}, f32[4,1,1,128,128]{4,3,2,1,0:T(8,128)}, u32[]{:S(2)}) copy-start(f32[4,1,1,128,128]{4,3,2,1,0:T(8,128)} %refs_2_.3) | copy-start | bytes 786436
  49.8 19.6 %copy-start.12 = (f32[4,1,1,64,128]{4,3,2,1,0:T(8,128)S(1)}, f32[4,1,1,64,128]{4,3,2,1,0:T(8,128)}, u32[]{:S(2)}) copy-start(f32[4,1,1,64,128]{4,3,2,1,0:T(8,128)} %refs_1_.3) | copy-start | bytes 393220
  69.6 86.7 %all-gather.16.cloned.1.call-start = ((), (), s32[]{:S(2)}) async-start(), calls=%async_computation.7 | async-start | bytes 1769472 | tf_op jit(solution)/shard_map/all_gather | solution.py:287
  94.6 103.3 %all-gather.22.cloned.1.call-start = ((), (), s32[]{:S(2)}) async-start(), calls=%async_computation.10 | async-start | bytes 1769472 | tf_op jit(solution)/shard_map/all_gather | solution.py:287
  94.7 1.3 copy-start
  96.0 18.2 %copy-start.1 = (f32[2624,128]{1,0:T(8,128)S(1)}, f32[2624,128]{1,0:T(8,128)}, u32[]{:S(2)}) copy-start(f32[2624,128]{1,0:T(8,128)} %all-gather.14.cloned.1.call-done) | copy-start | bytes 4030468
  133.5 1.3 copy-start.2
  134.9 20.6 %copy-start.3 = (f32[2688,128]{1,0:T(8,128)S(1)}, f32[2688,128]{1,0:T(8,128)}, u32[]{:S(2)}) copy-start(f32[2688,128]{1,0:T(8,128)} %all-gather.18.cloned.1.call-done) | copy-start | bytes 4128772
  177.5 1.3 copy-start.7
  180.9 0.8 copy-start.11
  181.7 16.0 %copy-start.8 = (f32[2304,128]{1,0:T(8,128)S(1)}, f32[2304,128]{1,0:T(8,128)}, u32[]{:S(2)}) copy-start(f32[2304,128]{1,0:T(8,128)} %all-gather.16.cloned.1.call-done) | copy-start | bytes 3538948
  181.7 16.0 %all-to-all-start.3 = ((f32[16,2,32,128]{3,2,1,0:T(8,128)}), f32[16,2,32,128]{3,2,1,0:T(8,128)S(1)}, u32[]{:S(2)}, u32[]{:S(2)}) async-start(f32[16,2,32,128]{3,2,1,0:T(8,128)} %copy-done.11), calls=%async_computation.3 | async-start | bytes 1048576 | tf_op jit(solution)/shard_map/all_to_all | solution.py:293
  185.4 50.9 %all-gather.20.cloned.1.call-start = ((), (), s32[]{:S(2)}) async-start(), calls=%async_computation.9 | async-start | bytes 1867776 | tf_op jit(solution)/shard_map/all_gather | solution.py:287
  217.9 1.3 copy-start.9
  256.5 1.3 copy-start.4
  257.8 17.0 %copy-start.5 = (f32[2432,128]{1,0:T(8,128)S(1)}, f32[2432,128]{1,0:T(8,128)}, u32[]{:S(2)}) copy-start(f32[2432,128]{1,0:T(8,128)} %all-gather.20.cloned.1.call-done) | copy-start | bytes 3735556
Sparse Core Ops, SparseCore 0:
  38.7 30.1 all-gather.13
  71.0 37.3 all-gather.17
  110.5 33.4 all-gather.15
  146.0 35.9 all-gather.21
  188.0 32.9 all-gather.19

commit v3 on v2

--- a/solution.py
+++ b/solution.py
@@ -308,7 +308,8 @@
         [(1, 1), (3, 1)],
         [(1, 0), (3, 0), (6, None)],
     ]
-    bundles = list(build_bundles(raw, held))
+    bundles = list(build_bundles(raw, held[:1])) + list(build_bundles(raw, held[1:]))
+    near, *bundles[1:] = lax.optimization_barrier((near, *bundles[1:]))
     parts = own_products(True, 0, parity, l_source, l_target, l_rows, near, far, l_tiles)
     in_tiles = tiles * height
     shared = [both(bundles[0])]
@@ -321,12 +322,10 @@
     for step, level in enumerate([2, 3, 2, 1, 0]):
         is_forward = step < 2
         mine = shared[step]
-        if step:
-            mine, value = after(mine, value)
+        if step + 2 < len(bundles):
+            later, value = after(bundles[step + 2], value)
+            shared.append(both(later))
         blocks = gather(value).reshape(prow, half, width)
-        if step + 2 < len(bundles):
-            later, blocks = after(bundles[step + 2], blocks)
-            shared.append(both(later))
         structure_at = in_tiles + width + nrhs + (level - 1 if is_forward else level) * STEP_ROWS
         parts = products(is_forward, shared[0], structure_at, blocks, mine, tiles, height)
         got = exchange(parts)

time: 289 us -> 283 us (0.979)
  the two profiles are of different devices: /device:TPU:32 before, /device:TPU:2 now
where the time goes in v3:
time: 283 us; the launch traced here: 282 us
  blocking collectives  215 us (76%)
  Pallas kernels  22 us (8%)
  waiting for transfers between devices  17.1 us (6%)
  between operations  13.3 us (5%)
  starting transfers between devices  7.77 us (3%)
  local copies, waits for them, and re-layouts  7.36 us (3%)
    all_gather x6, blocking collectives, gather(): lax.all_gather(value, 'prow', axis=0, tiled=True, axis_index_groups=groups)  128 us
    all_to_all x5, blocking collectives, exchange(): return lax.all_to_all(parts, 'pcol', 0, 0, tiled=True)  76.9 us
    pallas_call x16, Pallas kernels, call(): pl.pallas_call(kernel, grid=grid, out_shape=outs, in_specs=in_specs, out_...  22 us
    all_to_all x1, waiting for transfers between devices, exchange(): return lax.all_to_all(parts, 'pcol', 0, 0, tiled=True)  10.5 us
    all_gather x2, blocking collectives, both(): lax.all_gather(array, 'prow', axis=0, tiled=False, axis_index_groups=pairs)  10.2 us
    unnamed x32, local copies, waits for them, and re-layouts  7.35 us
    ppermute x1, waiting for transfers between devices, body(): far = lax.ppermute(near, 'prow', onward)  6.03 us
  transfers between devices with their start and end apart: 7, of which 2 were waited for; matrix products, arithmetic and copies ran while one was open for 0% of the time, Pallas kernels for 5%

profile of v3, /device:TPU:2, one launch (start us, length us, event | category | flops | bytes accessed | tf_op | source)
XLA Modules:
  0.0 282.4 jit_solution(2296628394379602732)
XLA Ops:
  6.5 0.0 all-gather.14.cloned.1.call-start
  6.5 1.6 shard_map.109
  8.2 27.5 %all-gather = f32[1024,128]{1,0:T(8,128)S(1)} all-gather(f32[64,128]{1,0:T(8,128)} %get-tuple-element.41.refs_6_), channel_id=2, replica_groups={{0,16,64,80,128,144,192,208,256,272,320,336,384,400,448,464},{32,48,96,..., dimensions={0}, use_global_device_ids=true | all-gather | bytes 557056 | tf_op jit(solution)/shard_map/all_gather | solution.py:290
  35.7 1.9 shard_map.110
  37.7 0.0 all-gather.14.cloned.1.call-update
  37.7 0.0 all-gather.16.cloned.1.call-start
  37.7 2.9 %collective-permute-start = (f32[16,64,128]{2,1,0:T(8,128)S(1)}, f32[16,64,128]{2,1,0:T(8,128)S(1)}, u32[]{:S(2)}, u32[]{:S(2)}) collective-permute-start(f32[16,64,128]{2,1,0:T(8,128)S(1)} %bitcast.42), channel_id=1, source_target_pairs={{0,32},{16,496},{32,64},{48,16},{64,96},{80,48},{96,128},{112,80},... | collective-permute-start | bytes 1572872 | tf_op jit(solution)/shard_map/ppermute | solution.py:303
  40.7 0.0 copy-start.4
  40.7 0.0 copy-start.13
  40.7 0.0 copy-start.14
  40.7 0.0 copy-start.15
  40.7 3.2 %shard_map.111 = (f32[1344,128]{1,0:T(8,128)}, f32[1152,128]{1,0:T(8,128)}, f32[1152,128]{1,0:T(8,128)}, f32[1216,128]{1,0:T(8,128)}) custom-call(f32[3,1024,128]{2,1,0:T(8,128)} %bitcast.32, f32[3,1024,128]{2,1,0:T(8,128)} %bitcast.48, f32[4,128,128]{2,1,0:T(8,128)} %bitcast.41, f32[4,128,128]{2,1,0:T(8,128)} %bitcast.50, f32[4,64,128]{2,1,0:T(8,128)} %bitcast.45, ...), custom_call_target="tpu_custom_call" | custom-call | flops 16777216 | bytes 1048576 | tf_op jit(solution)/shard_map/pallas_call | solution.py:60
  44.0 6.0 %collective-permute-done.refs_5_ = f32[16,64,128]{2,1,0:T(8,128)S(1)} collective-permute-done((f32[16,64,128]{2,1,0:T(8,128)S(1)}, f32[16,64,128]{2,1,0:T(8,128)S(1)}, u32[]{:S(2)}, u32[]{:S(2)}) %collective-permute-start) | collective-permute-done | bytes 524320 | tf_op jit(solution)/shard_map/ppermute | solution.py:303
  50.0 0.0 copy-done.4
  50.0 0.0 copy-done.13
  50.0 0.0 copy-done.14
  50.0 0.0 copy-done.15
  50.0 0.0 copy-start.10
  50.0 0.0 copy-start.12
  50.1 1.6 shard_map.112
  51.6 16.0 %all_to_all.30.refs_0_ = f32[16,64,128]{2,1,0:T(8,128)S(1)} all-to-all(f32[16,64,128]{2,1,0:T(8,128)S(1)} %shard_map.112), channel_id=1, replica_groups=mesh['prow'=32,'pcol'=16] {'pcol'}, dimensions={0} | all-to-all | bytes 1048576 | tf_op jit(solution)/shard_map/all_to_all | solution.py:293
  67.6 0.0 copy-done.10
  67.7 0.0 copy-done.12
  67.7 0.2 shard_map.113
  67.8 0.0 all-gather.16.cloned.1.call-update
  67.9 0.0 all-gather.18.cloned.1.call-start
  67.9 4.6 %all-gather.2 = f32[128,128]{1,0:T(8,128)S(1)} all-gather(f32[64,128]{1,0:T(8,128)S(1)} %shard_map.113), channel_id=4, replica_groups={{0,32},{16,48},{64,96},{80,112},{128,160},{144,176},{192,224},{208,240}..., dimensions={0}, use_global_device_ids=true | all-gather | bytes 98304 | tf_op jit(solution)/shard_map/all_gather | solution.py:287
  72.5 0.0 all-gather.18.cloned.1.call-update
  72.5 0.0 all-gather.20.cloned.1.call-start
  72.6 19.3 %all_gather.65.refs_2_ = f32[32,32,128]{2,1,0:T(8,128)S(1)} all-gather(f32[2,32,128]{2,1,0:T(8,128)S(1)} %constant_dynamic-slice_fusion.refs_1_), channel_id=1, replica_groups={{0,16,64,80,128,144,192,208,256,272,320,336,384,400,448,464},{32,48,96,..., dimensions={0}, use_global_device_ids=true | all-gather | bytes 557056 | tf_op jit(solution)/shard_map/all_gather | solution.py:290
  91.9 1.3 copy-done
  93.2 2.5 shard_map.114
  95.7 15.3 %all_to_all.31.refs_1_ = f32[16,2,32,128]{3,2,1,0:T(8,128)S(1)} all-to-all(f32[16,2,32,128]{3,2,1,0:T(8,128)S(1)} %shard_map.114), channel_id=1, replica_groups=mesh['prow'=32,'pcol'=16] {'pcol'}, dimensions={0} | all-to-all | bytes 1048576 | tf_op jit(solution)/shard_map/all_to_all | solution.py:293
  111.0 0.0 copy-done.1
  111.0 0.2 shard_map.115.refs_1_
  111.2 0.0 all-gather.20.cloned.1.call-update
  111.2 21.3 %all_gather.66.refs_2_ = f32[32,32,128]{2,1,0:T(8,128)S(1)} all-gather(f32[2,32,128]{2,1,0:T(8,128)S(1)} %shard_map.115.refs_1_), channel_id=1, replica_groups={{0,16,64,80,128,144,192,208,256,272,320,336,384,400,448,464},{32,48,96,..., dimensions={0}, use_global_device_ids=true | all-gather | bytes 557056 | tf_op jit(solution)/shard_map/all_gather | solution.py:290
  132.6 1.3 copy-done.2
  133.9 2.5 shard_map.116
  136.4 15.8 %all_to_all.32.refs_1_ = f32[16,2,32,128]{3,2,1,0:T(8,128)S(1)} all-to-all(f32[16,2,32,128]{3,2,1,0:T(8,128)S(1)} %shard_map.116), channel_id=1, replica_groups=mesh['prow'=32,'pcol'=16] {'pcol'}, dimensions={0} | all-to-all | bytes 1048576 | tf_op jit(solution)/shard_map/all_to_all | solution.py:293
  152.2 0.0 copy-done.3
  152.2 0.8 shard_map.117
  153.0 18.2 %all_gather.69.refs_2_ = f32[32,32,128]{2,1,0:T(8,128)S(1)} all-gather(f32[2,32,128]{2,1,0:T(8,128)S(1)} %get-tuple-element.57.refs_6_), channel_id=1, replica_groups={{0,16,64,80,128,144,192,208,256,272,320,336,384,400,448,464},{32,48,96,..., dimensions={0}, use_global_device_ids=true | all-gather | bytes 557056 | tf_op jit(solution)/shard_map/all_gather | solution.py:290
  171.2 1.3 copy-done.7
  172.5 2.1 shard_map.118
  174.5 0.0 copy-start.11
  174.6 0.8 copy-done.11
  175.4 4.7 %all-to-all-start.3 = ((f32[16,2,32,128]{3,2,1,0:T(8,128)}), f32[16,2,32,128]{3,2,1,0:T(8,128)S(1)}, u32[]{:S(2)}, u32[]{:S(2)}) async-start(f32[16,2,32,128]{3,2,1,0:T(8,128)} %copy-done.11), calls=%async_computation.3 | async-start | bytes 1048576 | tf_op jit(solution)/shard_map/all_to_all | solution.py:293
  180.0 0.0 all-gather.22.cloned.1.call-start
  180.1 0.5 all-gather.22.cloned.1.call-update
  180.6 10.5 %all-to-all-done.3.refs_0_ = f32[16,2,32,128]{3,2,1,0:T(8,128)S(1)} async-done(((f32[16,2,32,128]{3,2,1,0:T(8,128)}), f32[16,2,32,128]{3,2,1,0:T(8,128)S(1)}, u32[]{:S(2)}, u32[]{:S(2)}) %all-to-all-start.3) | async-done | bytes 524320 | tf_op jit(solution)/shard_map/all_to_all | solution.py:293
  191.1 0.2 shard_map.119.refs_5_
  191.2 23.5 %all_gather.72.refs_2_ = f32[32,32,128]{2,1,0:T(8,128)S(1)} all-gather(f32[2,32,128]{2,1,0:T(8,128)S(1)} %shard_map.119.refs_5_), channel_id=1, replica_groups={{0,16,64,80,128,144,192,208,256,272,320,336,384,400,448,464},{32,48,96,..., dimensions={0}, use_global_device_ids=true | all-gather | bytes 557056 | tf_op jit(solution)/shard_map/all_gather | solution.py:290
  214.7 1.3 copy-done.9
  216.0 2.1 shard_map.120
  218.1 14.8 %all_to_all.33.refs_0_ = f32[16,2,32,128]{3,2,1,0:T(8,128)S(1)} all-to-all(f32[16,2,32,128]{3,2,1,0:T(8,128)S(1)} %shard_map.120), channel_id=1, replica_groups=mesh['prow'=32,'pcol'=16] {'pcol'}, dimensions={0} | all-to-all | bytes 1048576 | tf_op jit(solution)/shard_map/all_to_all | solution.py:293
  232.9 0.2 shard_map.121.refs_4_
  233.1 18.0 %all_gather.75.refs_2_ = f32[32,32,128]{2,1,0:T(8,128)S(1)} all-gather(f32[2,32,128]{2,1,0:T(8,128)S(1)} %shard_map.121.refs_4_), channel_id=1, replica_groups={{0,16,64,80,128,144,192,208,256,272,320,336,384,400,448,464},{32,48,96,..., dimensions={0}, use_global_device_ids=true | all-gather | bytes 557056 | tf_op jit(solution)/shard_map/all_gather | solution.py:290
  251.1 1.3 copy-done.5
  252.4 2.1 shard_map.122
  254.4 15.0 %all_to_all.34.refs_1_ = f32[16,2,32,128]{3,2,1,0:T(8,128)S(1)} all-to-all(f32[16,2,32,128]{3,2,1,0:T(8,128)S(1)} %shard_map.122), channel_id=1, replica_groups=mesh['prow'=32,'pcol'=16] {'pcol'}, dimensions={0} | all-to-all | bytes 1048576 | tf_op jit(solution)/shard_map/all_to_all | solution.py:293
  269.4 0.2 shard_map.123
  269.6 5.6 %all-gather.7 = f32[8,2,32,128]{3,2,1,0:T(8,128)S(1)} all-gather(f32[4,2,32,128]{3,2,1,0:T(8,128)S(1)} %shard_map.123), channel_id=9, replica_groups={{0,32},{16,48},{64,96},{80,112},{128,160},{144,176},{192,224},{208,240}..., dimensions={0}, use_global_device_ids=true | all-gather | bytes 393216 | tf_op jit(solution)/shard_map/all_gather | solution.py:287
  275.2 0.7 shard_map.124
  (17 shorter events, 0.0 us)
Async XLA Ops:
  6.5 85.3 %all-gather.14.cloned.1.call-start = ((), (), s32[]{:S(2)}) async-start(), calls=%async_computation.6 | async-start | bytes 2015232 | tf_op jit(solution)/shard_map/all_gather | solution.py:287
  37.7 94.9 %all-gather.16.cloned.1.call-start = ((), (), s32[]{:S(2)}) async-start(), calls=%async_computation.7 | async-start | bytes 2064384 | tf_op jit(solution)/shard_map/all_gather | solution.py:287
  37.7 12.3 %collective-permute-start = (f32[16,64,128]{2,1,0:T(8,128)S(1)}, f32[16,64,128]{2,1,0:T(8,128)S(1)}, u32[]{:S(2)}, u32[]{:S(2)}) collective-permute-start(f32[16,64,128]{2,1,0:T(8,128)S(1)} %bitcast.42), channel_id=1, source_target_pairs={{0,32},{16,496},{32,64},{48,16},{64,96},{80,48},{96,128},{112,80},... | collective-permute-start | bytes 1572872 | tf_op jit(solution)/shard_map/ppermute | solution.py:303
  40.7 9.3 %copy-start.4 = (f32[3,1,1,16,64,128]{5,4,3,2,1,0:T(8,128)S(1)}, f32[3,1,1,16,64,128]{5,4,3,2,1,0:T(8,128)}, u32[]{:S(2)}) copy-start(f32[3,1,1,16,64,128]{5,4,3,2,1,0:T(8,128)} %refs_6_.1) | copy-start | bytes 4718596
  40.7 9.3 %copy-start.13 = (s32[3,1,1,16,64]{4,3,2,1,0:T(8,128)S(1)}, s32[3,1,1,16,64]{4,3,2,1,0:T(8,128)}, u32[]{:S(2)}) copy-start(s32[3,1,1,16,64]{4,3,2,1,0:T(8,128)} %refs_3_.1) | copy-start | bytes 36868
  40.7 9.3 %copy-start.14 = (s32[3,1,1,16]{3,2,1,0:T(1,128)S(1)}, s32[3,1,1,16]{3,2,1,0:T(1,128)}, u32[]{:S(2)}) copy-start(s32[3,1,1,16]{3,2,1,0:T(1,128)} %refs_1_.2) | copy-start | bytes 580
  40.7 9.3 %copy-start.15 = (s32[3,1,1,16]{3,2,1,0:T(1,128)S(1)}, s32[3,1,1,16]{3,2,1,0:T(1,128)}, u32[]{:S(2)}) copy-start(s32[3,1,1,16]{3,2,1,0:T(1,128)} %refs_2_.2) | copy-start | bytes 580
  50.0 17.6 %copy-start.10 = (f32[4,1,1,128,128]{4,3,2,1,0:T(8,128)S(1)}, f32[4,1,1,128,128]{4,3,2,1,0:T(8,128)}, u32[]{:S(2)}) copy-start(f32[4,1,1,128,128]{4,3,2,1,0:T(8,128)} %refs_2_.3) | copy-start | bytes 786436
  50.0 17.6 %copy-start.12 = (f32[4,1,1,64,128]{4,3,2,1,0:T(8,128)S(1)}, f32[4,1,1,64,128]{4,3,2,1,0:T(8,128)}, u32[]{:S(2)}) copy-start(f32[4,1,1,64,128]{4,3,2,1,0:T(8,128)} %refs_1_.3) | copy-start | bytes 393220
  67.9 103.3 %all-gather.18.cloned.1.call-start = ((), (), s32[]{:S(2)}) async-start(), calls=%async_computation.8 | async-start | bytes 1769472 | tf_op jit(solution)/shard_map/all_gather | solution.py:287
  72.5 142.2 %all-gather.20.cloned.1.call-start = ((), (), s32[]{:S(2)}) async-start(), calls=%async_computation.9 | async-start | bytes 1769472 | tf_op jit(solution)/shard_map/all_gather | solution.py:287
  91.9 1.3 copy-start
  93.2 17.8 %copy-start.1 = (f32[2624,128]{1,0:T(8,128)S(1)}, f32[2624,128]{1,0:T(8,128)}, u32[]{:S(2)}) copy-start(f32[2624,128]{1,0:T(8,128)} %all-gather.14.cloned.1.call-done) | copy-start | bytes 4030468
  132.6 1.3 copy-start.2
  133.9 18.3 %copy-start.3 = (f32[2688,128]{1,0:T(8,128)S(1)}, f32[2688,128]{1,0:T(8,128)}, u32[]{:S(2)}) copy-start(f32[2688,128]{1,0:T(8,128)} %all-gather.16.cloned.1.call-done) | copy-start | bytes 4128772
  171.2 1.3 copy-start.7
  174.5 0.8 copy-start.11
  175.3 15.7 %copy-start.8 = (f32[2304,128]{1,0:T(8,128)S(1)}, f32[2304,128]{1,0:T(8,128)}, u32[]{:S(2)}) copy-start(f32[2304,128]{1,0:T(8,128)} %all-gather.18.cloned.1.call-done) | copy-start | bytes 3538948
  175.4 15.7 %all-to-all-start.3 = ((f32[16,2,32,128]{3,2,1,0:T(8,128)}), f32[16,2,32,128]{3,2,1,0:T(8,128)S(1)}, u32[]{:S(2)}, u32[]{:S(2)}) async-start(f32[16,2,32,128]{3,2,1,0:T(8,128)} %copy-done.11), calls=%async_computation.3 | async-start | bytes 1048576 | tf_op jit(solution)/shard_map/all_to_all | solution.py:293
  180.0 71.0 %all-gather.22.cloned.1.call-start = ((), (), s32[]{:S(2)}) async-start(), calls=%async_computation.10 | async-start | bytes 1867776 | tf_op jit(solution)/shard_map/all_gather | solution.py:287
  214.7 1.3 copy-start.9
  251.1 1.3 copy-start.5
  252.4 17.0 %copy-start.6 = (f32[2432,128]{1,0:T(8,128)S(1)}, f32[2432,128]{1,0:T(8,128)}, u32[]{:S(2)}) copy-start(f32[2432,128]{1,0:T(8,128)} %all-gather.22.cloned.1.call-done) | copy-start | bytes 3735556
Sparse Core Ops, SparseCore 0:
  37.8 30.9 all-gather.13
  70.8 36.9 all-gather.15
  109.9 33.4 all-gather.17
  145.4 33.8 all-gather.19
  182.6 34.5 all-gather.21

commit v4 on v3

--- a/solution.py
+++ b/solution.py
@@ -73,9 +73,9 @@
     tiles = tiles_ref.shape[0]
     rows = rows_ref[...]
     rows = jnp.concatenate([rows, rows], axis=1)
-    for first in range(0, tiles, 4):
+    for first in range(0, tiles, 8):
         held = []
-        for k in range(first, first + 4):
+        for k in range(first, first + 8):
             source = source_ref[level, 0, 0, k]
             at = 2 * (source >> 2) + (source & 1)
             is_near = ((source >> 1) & 1) == parity_ref[0]
@@ -115,8 +115,8 @@
     def scalar(row, kind, k):
         return at_ref[row, tiles + kind, first_lane + k].astype(jnp.int32)
 
-    for first in range(0, 2 * tiles, 8):
-        group = range(first, first + 8)
+    for first in range(0, 2 * tiles, 16):
+        group = range(first, first + 16)
         held = []
         for t in group:
             row, k = divmod(t, tiles)

time: 283 us -> 283 us (level)
  no operation moved by 1% of the time
where the time goes in v4:
time: 283 us; the launch traced here: 282 us
  blocking collectives  215 us (76%)
  Pallas kernels  21.1 us (7%)
  waiting for transfers between devices  17.1 us (6%)
  between operations  13.3 us (5%)
  starting transfers between devices  7.75 us (3%)
  local copies, waits for them, and re-layouts  7.36 us (3%)
    all_gather x6, blocking collectives, gather(): lax.all_gather(value, 'prow', axis=0, tiled=True, axis_index_groups=groups)  129 us
    all_to_all x5, blocking collectives, exchange(): return lax.all_to_all(parts, 'pcol', 0, 0, tiled=True)  76.2 us
    pallas_call x16, Pallas kernels, call(): pl.pallas_call(kernel, grid=grid, out_shape=outs, in_specs=in_specs, out_...  21.1 us
    all_to_all x1, waiting for transfers between devices, exchange(): return lax.all_to_all(parts, 'pcol', 0, 0, tiled=True)  10.5 us
    all_gather x2, blocking collectives, both(): lax.all_gather(array, 'prow', axis=0, tiled=False, axis_index_groups=pairs)  10.2 us
    unnamed x32, local copies, waits for them, and re-layouts  7.35 us
    ppermute x1, waiting for transfers between devices, body(): far = lax.ppermute(near, 'prow', onward)  6.03 us
  transfers between devices with their start and end apart: 7, of which 2 were waited for; matrix products, arithmetic and copies ran while one was open for 0% of the time, Pallas kernels for 5%

profile of v4, /device:TPU:2, one launch (start us, length us, event | category | flops | bytes accessed | tf_op | source)
XLA Modules:
  0.0 281.8 jit_solution(5341187098918874822)
XLA Ops:
  6.5 0.0 all-gather.14.cloned.1.call-start
  6.5 1.6 shard_map.109
  8.2 27.5 %all-gather = f32[1024,128]{1,0:T(8,128)S(1)} all-gather(f32[64,128]{1,0:T(8,128)} %get-tuple-element.41.refs_6_), channel_id=2, replica_groups={{0,16,64,80,128,144,192,208,256,272,320,336,384,400,448,464},{32,48,96,..., dimensions={0}, use_global_device_ids=true | all-gather | bytes 557056 | tf_op jit(solution)/shard_map/all_gather | solution.py:290
  35.7 1.9 shard_map.110
  37.7 0.0 all-gather.14.cloned.1.call-update
  37.7 0.0 all-gather.16.cloned.1.call-start
  37.7 2.9 %collective-permute-start = (f32[16,64,128]{2,1,0:T(8,128)S(1)}, f32[16,64,128]{2,1,0:T(8,128)S(1)}, u32[]{:S(2)}, u32[]{:S(2)}) collective-permute-start(f32[16,64,128]{2,1,0:T(8,128)S(1)} %bitcast.42), channel_id=1, source_target_pairs={{0,32},{16,496},{32,64},{48,16},{64,96},{80,48},{96,128},{112,80},... | collective-permute-start | bytes 1572872 | tf_op jit(solution)/shard_map/ppermute | solution.py:303
  40.7 0.0 copy-start.4
  40.7 0.0 copy-start.13
  40.7 0.0 copy-start.14
  40.7 0.0 copy-start.15
  40.7 3.2 %shard_map.111 = (f32[1344,128]{1,0:T(8,128)}, f32[1152,128]{1,0:T(8,128)}, f32[1152,128]{1,0:T(8,128)}, f32[1216,128]{1,0:T(8,128)}) custom-call(f32[3,1024,128]{2,1,0:T(8,128)} %bitcast.32, f32[3,1024,128]{2,1,0:T(8,128)} %bitcast.48, f32[4,128,128]{2,1,0:T(8,128)} %bitcast.41, f32[4,128,128]{2,1,0:T(8,128)} %bitcast.50, f32[4,64,128]{2,1,0:T(8,128)} %bitcast.45, ...), custom_call_target="tpu_custom_call" | custom-call | flops 16777216 | bytes 1048576 | tf_op jit(solution)/shard_map/pallas_call | solution.py:60
  44.0 6.0 %collective-permute-done.refs_5_ = f32[16,64,128]{2,1,0:T(8,128)S(1)} collective-permute-done((f32[16,64,128]{2,1,0:T(8,128)S(1)}, f32[16,64,128]{2,1,0:T(8,128)S(1)}, u32[]{:S(2)}, u32[]{:S(2)}) %collective-permute-start) | collective-permute-done | bytes 524320 | tf_op jit(solution)/shard_map/ppermute | solution.py:303
  50.0 0.0 copy-done.4
  50.0 0.0 copy-done.13
  50.0 0.0 copy-done.14
  50.0 0.0 copy-done.15
  50.0 0.0 copy-start.10
  50.0 0.0 copy-start.12
  50.1 1.4 shard_map.112
  51.5 16.0 %all_to_all.30.refs_0_ = f32[16,64,128]{2,1,0:T(8,128)S(1)} all-to-all(f32[16,64,128]{2,1,0:T(8,128)S(1)} %shard_map.112), channel_id=1, replica_groups=mesh['prow'=32,'pcol'=16] {'pcol'}, dimensions={0} | all-to-all | bytes 1048576 | tf_op jit(solution)/shard_map/all_to_all | solution.py:293
  67.5 0.0 copy-done.10
  67.5 0.0 copy-done.12
  67.5 0.2 shard_map.113
  67.7 0.0 all-gather.16.cloned.1.call-update
  67.7 0.0 all-gather.18.cloned.1.call-start
  67.8 4.6 %all-gather.2 = f32[128,128]{1,0:T(8,128)S(1)} all-gather(f32[64,128]{1,0:T(8,128)S(1)} %shard_map.113), channel_id=4, replica_groups={{0,32},{16,48},{64,96},{80,112},{128,160},{144,176},{192,224},{208,240}..., dimensions={0}, use_global_device_ids=true | all-gather | bytes 98304 | tf_op jit(solution)/shard_map/all_gather | solution.py:287
  72.4 0.0 all-gather.18.cloned.1.call-update
  72.4 0.0 all-gather.20.cloned.1.call-start
  72.4 19.4 %all_gather.65.refs_2_ = f32[32,32,128]{2,1,0:T(8,128)S(1)} all-gather(f32[2,32,128]{2,1,0:T(8,128)S(1)} %constant_dynamic-slice_fusion.refs_1_), channel_id=1, replica_groups={{0,16,64,80,128,144,192,208,256,272,320,336,384,400,448,464},{32,48,96,..., dimensions={0}, use_global_device_ids=true | all-gather | bytes 557056 | tf_op jit(solution)/shard_map/all_gather | solution.py:290
  91.8 1.3 copy-done
  93.1 2.5 shard_map.114
  95.6 15.3 %all_to_all.31.refs_1_ = f32[16,2,32,128]{3,2,1,0:T(8,128)S(1)} all-to-all(f32[16,2,32,128]{3,2,1,0:T(8,128)S(1)} %shard_map.114), channel_id=1, replica_groups=mesh['prow'=32,'pcol'=16] {'pcol'}, dimensions={0} | all-to-all | bytes 1048576 | tf_op jit(solution)/shard_map/all_to_all | solution.py:293
  110.9 0.0 copy-done.1
  110.9 0.2 shard_map.115.refs_1_
  111.1 0.0 all-gather.20.cloned.1.call-update
  111.1 22.1 %all_gather.66.refs_2_ = f32[32,32,128]{2,1,0:T(8,128)S(1)} all-gather(f32[2,32,128]{2,1,0:T(8,128)S(1)} %shard_map.115.refs_1_), channel_id=1, replica_groups={{0,16,64,80,128,144,192,208,256,272,320,336,384,400,448,464},{32,48,96,..., dimensions={0}, use_global_device_ids=true | all-gather | bytes 557056 | tf_op jit(solution)/shard_map/all_gather | solution.py:290
  133.1 1.3 copy-done.2
  134.5 2.5 shard_map.116
  137.0 15.0 %all_to_all.32.refs_1_ = f32[16,2,32,128]{3,2,1,0:T(8,128)S(1)} all-to-all(f32[16,2,32,128]{3,2,1,0:T(8,128)S(1)} %shard_map.116), channel_id=1, replica_groups=mesh['prow'=32,'pcol'=16] {'pcol'}, dimensions={0} | all-to-all | bytes 1048576 | tf_op jit(solution)/shard_map/all_to_all | solution.py:293
  151.9 0.0 copy-done.3
  151.9 0.8 shard_map.117
  152.8 18.5 %all_gather.69.refs_2_ = f32[32,32,128]{2,1,0:T(8,128)S(1)} all-gather(f32[2,32,128]{2,1,0:T(8,128)S(1)} %get-tuple-element.57.refs_6_), channel_id=1, replica_groups={{0,16,64,80,128,144,192,208,256,272,320,336,384,400,448,464},{32,48,96,..., dimensions={0}, use_global_device_ids=true | all-gather | bytes 557056 | tf_op jit(solution)/shard_map/all_gather | solution.py:290
  171.3 1.3 copy-done.7
  172.6 1.8 shard_map.118
  174.4 0.8 copy-done.11
  175.2 4.6 %all-to-all-start.3 = ((f32[16,2,32,128]{3,2,1,0:T(8,128)}), f32[16,2,32,128]{3,2,1,0:T(8,128)S(1)}, u32[]{:S(2)}, u32[]{:S(2)}) async-start(f32[16,2,32,128]{3,2,1,0:T(8,128)} %copy-done.11), calls=%async_computation.3 | async-start | bytes 1048576 | tf_op jit(solution)/shard_map/all_to_all | solution.py:293
  179.9 0.0 all-gather.22.cloned.1.call-start
  179.9 0.5 all-gather.22.cloned.1.call-update
  180.5 10.5 %all-to-all-done.3.refs_0_ = f32[16,2,32,128]{3,2,1,0:T(8,128)S(1)} async-done(((f32[16,2,32,128]{3,2,1,0:T(8,128)}), f32[16,2,32,128]{3,2,1,0:T(8,128)S(1)}, u32[]{:S(2)}, u32[]{:S(2)}) %all-to-all-start.3) | async-done | bytes 524320 | tf_op jit(solution)/shard_map/all_to_all | solution.py:293
  190.9 0.0 copy-done.8
  190.9 0.2 shard_map.119.refs_5_
  191.1 22.9 %all_gather.72.refs_2_ = f32[32,32,128]{2,1,0:T(8,128)S(1)} all-gather(f32[2,32,128]{2,1,0:T(8,128)S(1)} %shard_map.119.refs_5_), channel_id=1, replica_groups={{0,16,64,80,128,144,192,208,256,272,320,336,384,400,448,464},{32,48,96,..., dimensions={0}, use_global_device_ids=true | all-gather | bytes 557056 | tf_op jit(solution)/shard_map/all_gather | solution.py:290
  214.0 1.3 copy-done.9
  215.2 1.9 shard_map.120
  217.1 15.0 %all_to_all.33.refs_0_ = f32[16,2,32,128]{3,2,1,0:T(8,128)S(1)} all-to-all(f32[16,2,32,128]{3,2,1,0:T(8,128)S(1)} %shard_map.120), channel_id=1, replica_groups=mesh['prow'=32,'pcol'=16] {'pcol'}, dimensions={0} | all-to-all | bytes 1048576 | tf_op jit(solution)/shard_map/all_to_all | solution.py:293
  232.1 0.2 shard_map.121.refs_4_
  232.3 18.4 %all_gather.75.refs_2_ = f32[32,32,128]{2,1,0:T(8,128)S(1)} all-gather(f32[2,32,128]{2,1,0:T(8,128)S(1)} %shard_map.121.refs_4_), channel_id=1, replica_groups={{0,16,64,80,128,144,192,208,256,272,320,336,384,400,448,464},{32,48,96,..., dimensions={0}, use_global_device_ids=true | all-gather | bytes 557056 | tf_op jit(solution)/shard_map/all_gather | solution.py:290
  250.7 1.3 copy-done.5
  252.0 1.9 shard_map.122
  253.9 14.9 %all_to_all.34.refs_1_ = f32[16,2,32,128]{3,2,1,0:T(8,128)S(1)} all-to-all(f32[16,2,32,128]{3,2,1,0:T(8,128)S(1)} %shard_map.122), channel_id=1, replica_groups=mesh['prow'=32,'pcol'=16] {'pcol'}, dimensions={0} | all-to-all | bytes 1048576 | tf_op jit(solution)/shard_map/all_to_all | solution.py:293
  268.8 0.2 shard_map.123
  269.0 5.6 %all-gather.7 = f32[8,2,32,128]{3,2,1,0:T(8,128)S(1)} all-gather(f32[4,2,32,128]{3,2,1,0:T(8,128)S(1)} %shard_map.123), channel_id=9, replica_groups={{0,32},{16,48},{64,96},{80,112},{128,160},{144,176},{192,224},{208,240}..., dimensions={0}, use_global_device_ids=true | all-gather | bytes 393216 | tf_op jit(solution)/shard_map/all_gather | solution.py:287
  274.6 0.7 shard_map.124
  (17 shorter events, 0.0 us)
Async XLA Ops:
  6.5 85.3 %all-gather.14.cloned.1.call-start = ((), (), s32[]{:S(2)}) async-start(), calls=%async_computation.6 | async-start | bytes 2015232 | tf_op jit(solution)/shard_map/all_gather | solution.py:287
  37.7 95.5 %all-gather.16.cloned.1.call-start = ((), (), s32[]{:S(2)}) async-start(), calls=%async_computation.7 | async-start | bytes 2064384 | tf_op jit(solution)/shard_map/all_gather | solution.py:287
  37.7 12.3 %collective-permute-start = (f32[16,64,128]{2,1,0:T(8,128)S(1)}, f32[16,64,128]{2,1,0:T(8,128)S(1)}, u32[]{:S(2)}, u32[]{:S(2)}) collective-permute-start(f32[16,64,128]{2,1,0:T(8,128)S(1)} %bitcast.42), channel_id=1, source_target_pairs={{0,32},{16,496},{32,64},{48,16},{64,96},{80,48},{96,128},{112,80},... | collective-permute-start | bytes 1572872 | tf_op jit(solution)/shard_map/ppermute | solution.py:303
  40.7 9.3 %copy-start.4 = (f32[3,1,1,16,64,128]{5,4,3,2,1,0:T(8,128)S(1)}, f32[3,1,1,16,64,128]{5,4,3,2,1,0:T(8,128)}, u32[]{:S(2)}) copy-start(f32[3,1,1,16,64,128]{5,4,3,2,1,0:T(8,128)} %refs_6_.1) | copy-start | bytes 4718596
  40.7 9.3 %copy-start.13 = (s32[3,1,1,16,64]{4,3,2,1,0:T(8,128)S(1)}, s32[3,1,1,16,64]{4,3,2,1,0:T(8,128)}, u32[]{:S(2)}) copy-start(s32[3,1,1,16,64]{4,3,2,1,0:T(8,128)} %refs_3_.1) | copy-start | bytes 36868
  40.7 9.3 %copy-start.14 = (s32[3,1,1,16]{3,2,1,0:T(1,128)S(1)}, s32[3,1,1,16]{3,2,1,0:T(1,128)}, u32[]{:S(2)}) copy-start(s32[3,1,1,16]{3,2,1,0:T(1,128)} %refs_1_.2) | copy-start | bytes 580
  40.7 9.3 %copy-start.15 = (s32[3,1,1,16]{3,2,1,0:T(1,128)S(1)}, s32[3,1,1,16]{3,2,1,0:T(1,128)}, u32[]{:S(2)}) copy-start(s32[3,1,1,16]{3,2,1,0:T(1,128)} %refs_2_.2) | copy-start | bytes 580
  50.0 17.5 %copy-start.10 = (f32[4,1,1,128,128]{4,3,2,1,0:T(8,128)S(1)}, f32[4,1,1,128,128]{4,3,2,1,0:T(8,128)}, u32[]{:S(2)}) copy-start(f32[4,1,1,128,128]{4,3,2,1,0:T(8,128)} %refs_2_.3) | copy-start | bytes 786436
  50.0 17.5 %copy-start.12 = (f32[4,1,1,64,128]{4,3,2,1,0:T(8,128)S(1)}, f32[4,1,1,64,128]{4,3,2,1,0:T(8,128)}, u32[]{:S(2)}) copy-start(f32[4,1,1,64,128]{4,3,2,1,0:T(8,128)} %refs_1_.3) | copy-start | bytes 393220
  67.7 103.6 %all-gather.18.cloned.1.call-start = ((), (), s32[]{:S(2)}) async-start(), calls=%async_computation.8 | async-start | bytes 1769472 | tf_op jit(solution)/shard_map/all_gather | solution.py:287
  72.4 141.6 %all-gather.20.cloned.1.call-start = ((), (), s32[]{:S(2)}) async-start(), calls=%async_computation.9 | async-start | bytes 1769472 | tf_op jit(solution)/shard_map/all_gather | solution.py:287
  91.8 1.3 copy-start
  93.1 17.8 %copy-start.1 = (f32[2624,128]{1,0:T(8,128)S(1)}, f32[2624,128]{1,0:T(8,128)}, u32[]{:S(2)}) copy-start(f32[2624,128]{1,0:T(8,128)} %all-gather.14.cloned.1.call-done) | copy-start | bytes 4030468
  133.1 1.3 copy-start.2
  134.5 17.5 %copy-start.3 = (f32[2688,128]{1,0:T(8,128)S(1)}, f32[2688,128]{1,0:T(8,128)}, u32[]{:S(2)}) copy-start(f32[2688,128]{1,0:T(8,128)} %all-gather.16.cloned.1.call-done) | copy-start | bytes 4128772
  171.3 1.3 copy-start.7
  174.4 0.8 copy-start.11
  175.2 15.7 %copy-start.8 = (f32[2304,128]{1,0:T(8,128)S(1)}, f32[2304,128]{1,0:T(8,128)}, u32[]{:S(2)}) copy-start(f32[2304,128]{1,0:T(8,128)} %all-gather.18.cloned.1.call-done) | copy-start | bytes 3538948
  175.2 15.7 %all-to-all-start.3 = ((f32[16,2,32,128]{3,2,1,0:T(8,128)}), f32[16,2,32,128]{3,2,1,0:T(8,128)S(1)}, u32[]{:S(2)}, u32[]{:S(2)}) async-start(f32[16,2,32,128]{3,2,1,0:T(8,128)} %copy-done.11), calls=%async_computation.3 | async-start | bytes 1048576 | tf_op jit(solution)/shard_map/all_to_all | solution.py:293
  179.9 70.8 %all-gather.22.cloned.1.call-start = ((), (), s32[]{:S(2)}) async-start(), calls=%async_computation.10 | async-start | bytes 1867776 | tf_op jit(solution)/shard_map/all_gather | solution.py:287
  214.0 1.3 copy-start.9
  250.7 1.3 copy-start.5
  252.0 16.8 %copy-start.6 = (f32[2432,128]{1,0:T(8,128)S(1)}, f32[2432,128]{1,0:T(8,128)}, u32[]{:S(2)}) copy-start(f32[2432,128]{1,0:T(8,128)} %all-gather.22.cloned.1.call-done) | copy-start | bytes 3735556
Sparse Core Ops, SparseCore 0:
  37.8 30.9 all-gather.13
  70.8 37.0 all-gather.15
  110.0 33.4 all-gather.17
  145.5 33.8 all-gather.19
  182.5 34.4 all-gather.21

commit v5 on v4

--- a/solution.py
+++ b/solution.py
@@ -73,9 +73,9 @@
     tiles = tiles_ref.shape[0]
     rows = rows_ref[...]
     rows = jnp.concatenate([rows, rows], axis=1)
-    for first in range(0, tiles, 8):
+    for first in range(0, tiles, 16):
         held = []
-        for k in range(first, first + 8):
+        for k in range(first, first + 16):
             source = source_ref[level, 0, 0, k]
             at = 2 * (source >> 2) + (source & 1)
             is_near = ((source >> 1) & 1) == parity_ref[0]
@@ -115,8 +115,8 @@
     def scalar(row, kind, k):
         return at_ref[row, tiles + kind, first_lane + k].astype(jnp.int32)
 
-    for first in range(0, 2 * tiles, 16):
-        group = range(first, first + 16)
+    for first in range(0, 2 * tiles, 32):
+        group = range(first, first + 32)
         held = []
         for t in group:
             row, k = divmod(t, tiles)

time: 283 us -> 282 us (level)
  no operation moved by 1% of the time
where the time goes in v5:
time: 282 us; the launch traced here: 281 us
  blocking collectives  215 us (76%)
  Pallas kernels  21.1 us (7%)
  waiting for transfers between devices  17.1 us (6%)
  between operations  13.3 us (5%)
  starting transfers between devices  7.79 us (3%)
  local copies, waits for them, and re-layouts  7.36 us (3%)
    all_gather x6, blocking collectives, gather(): lax.all_gather(value, 'prow', axis=0, tiled=True, axis_index_groups=groups)  128 us
    all_to_all x5, blocking collectives, exchange(): return lax.all_to_all(parts, 'pcol', 0, 0, tiled=True)  76.5 us
    pallas_call x16, Pallas kernels, call(): pl.pallas_call(kernel, grid=grid, out_shape=outs, in_specs=in_specs, out_...  21.1 us
    all_to_all x1, waiting for transfers between devices, exchange(): return lax.all_to_all(parts, 'pcol', 0, 0, tiled=True)  10.5 us
    all_gather x2, blocking collectives, both(): lax.all_gather(array, 'prow', axis=0, tiled=False, axis_index_groups=pairs)  10.2 us
    unnamed x32, local copies, waits for them, and re-layouts  7.35 us
    ppermute x1, waiting for transfers between devices, body(): far = lax.ppermute(near, 'prow', onward)  6.03 us
  transfers between devices with their start and end apart: 7, of which 2 were waited for; matrix products, arithmetic and copies ran while one was open for 0% of the time, Pallas kernels for 5%

profile of v5, /device:TPU:2, one launch (start us, length us, event | category | flops | bytes accessed | tf_op | source)
XLA Modules:
  0.0 281.4 jit_solution(6499283314766883821)
XLA Ops:
  6.5 0.0 all-gather.14.cloned.1.call-start
  6.5 1.6 shard_map.109
  8.2 27.5 %all-gather = f32[1024,128]{1,0:T(8,128)S(1)} all-gather(f32[64,128]{1,0:T(8,128)} %get-tuple-element.41.refs_6_), channel_id=2, replica_groups={{0,16,64,80,128,144,192,208,256,272,320,336,384,400,448,464},{32,48,96,..., dimensions={0}, use_global_device_ids=true | all-gather | bytes 557056 | tf_op jit(solution)/shard_map/all_gather | solution.py:290
  35.7 1.9 shard_map.110
  37.7 0.0 all-gather.14.cloned.1.call-update
  37.7 0.0 all-gather.16.cloned.1.call-start
  37.7 2.9 %collective-permute-start = (f32[16,64,128]{2,1,0:T(8,128)S(1)}, f32[16,64,128]{2,1,0:T(8,128)S(1)}, u32[]{:S(2)}, u32[]{:S(2)}) collective-permute-start(f32[16,64,128]{2,1,0:T(8,128)S(1)} %bitcast.42), channel_id=1, source_target_pairs={{0,32},{16,496},{32,64},{48,16},{64,96},{80,48},{96,128},{112,80},... | collective-permute-start | bytes 1572872 | tf_op jit(solution)/shard_map/ppermute | solution.py:303
  40.7 0.0 copy-start.4
  40.7 0.0 copy-start.13
  40.7 0.0 copy-start.14
  40.7 0.0 copy-start.15
  40.7 3.2 %shard_map.111 = (f32[1344,128]{1,0:T(8,128)}, f32[1152,128]{1,0:T(8,128)}, f32[1152,128]{1,0:T(8,128)}, f32[1216,128]{1,0:T(8,128)}) custom-call(f32[3,1024,128]{2,1,0:T(8,128)} %bitcast.32, f32[3,1024,128]{2,1,0:T(8,128)} %bitcast.48, f32[4,128,128]{2,1,0:T(8,128)} %bitcast.41, f32[4,128,128]{2,1,0:T(8,128)} %bitcast.50, f32[4,64,128]{2,1,0:T(8,128)} %bitcast.45, ...), custom_call_target="tpu_custom_call" | custom-call | flops 16777216 | bytes 1048576 | tf_op jit(solution)/shard_map/pallas_call | solution.py:60
  44.0 6.0 %collective-permute-done.refs_5_ = f32[16,64,128]{2,1,0:T(8,128)S(1)} collective-permute-done((f32[16,64,128]{2,1,0:T(8,128)S(1)}, f32[16,64,128]{2,1,0:T(8,128)S(1)}, u32[]{:S(2)}, u32[]{:S(2)}) %collective-permute-start) | collective-permute-done | bytes 524320 | tf_op jit(solution)/shard_map/ppermute | solution.py:303
  50.0 0.0 copy-done.4
  50.0 0.0 copy-done.13
  50.0 0.0 copy-done.14
  50.0 0.0 copy-done.15
  50.0 0.0 copy-start.10
  50.0 0.0 copy-start.12
  50.1 1.4 shard_map.112
  51.5 16.0 %all_to_all.30.refs_0_ = f32[16,64,128]{2,1,0:T(8,128)S(1)} all-to-all(f32[16,64,128]{2,1,0:T(8,128)S(1)} %shard_map.112), channel_id=1, replica_groups=mesh['prow'=32,'pcol'=16] {'pcol'}, dimensions={0} | all-to-all | bytes 1048576 | tf_op jit(solution)/shard_map/all_to_all | solution.py:293
  67.5 0.0 copy-done.10
  67.5 0.0 copy-done.12
  67.5 0.2 shard_map.113
  67.7 0.0 all-gather.16.cloned.1.call-update
  67.7 0.0 all-gather.18.cloned.1.call-start
  67.8 4.6 %all-gather.2 = f32[128,128]{1,0:T(8,128)S(1)} all-gather(f32[64,128]{1,0:T(8,128)S(1)} %shard_map.113), channel_id=4, replica_groups={{0,32},{16,48},{64,96},{80,112},{128,160},{144,176},{192,224},{208,240}..., dimensions={0}, use_global_device_ids=true | all-gather | bytes 98304 | tf_op jit(solution)/shard_map/all_gather | solution.py:287
  72.4 0.0 all-gather.18.cloned.1.call-update
  72.4 0.0 all-gather.20.cloned.1.call-start
  72.4 19.4 %all_gather.65.refs_2_ = f32[32,32,128]{2,1,0:T(8,128)S(1)} all-gather(f32[2,32,128]{2,1,0:T(8,128)S(1)} %constant_dynamic-slice_fusion.refs_1_), channel_id=1, replica_groups={{0,16,64,80,128,144,192,208,256,272,320,336,384,400,448,464},{32,48,96,..., dimensions={0}, use_global_device_ids=true | all-gather | bytes 557056 | tf_op jit(solution)/shard_map/all_gather | solution.py:290
  91.8 1.3 copy-done
  93.1 2.5 shard_map.114
  95.6 15.3 %all_to_all.31.refs_1_ = f32[16,2,32,128]{3,2,1,0:T(8,128)S(1)} all-to-all(f32[16,2,32,128]{3,2,1,0:T(8,128)S(1)} %shard_map.114), channel_id=1, replica_groups=mesh['prow'=32,'pcol'=16] {'pcol'}, dimensions={0} | all-to-all | bytes 1048576 | tf_op jit(solution)/shard_map/all_to_all | solution.py:293
  110.9 0.0 copy-done.1
  110.9 0.2 shard_map.115.refs_1_
  111.1 0.0 all-gather.20.cloned.1.call-update
  111.1 22.2 %all_gather.66.refs_2_ = f32[32,32,128]{2,1,0:T(8,128)S(1)} all-gather(f32[2,32,128]{2,1,0:T(8,128)S(1)} %shard_map.115.refs_1_), channel_id=1, replica_groups={{0,16,64,80,128,144,192,208,256,272,320,336,384,400,448,464},{32,48,96,..., dimensions={0}, use_global_device_ids=true | all-gather | bytes 557056 | tf_op jit(solution)/shard_map/all_gather | solution.py:290
  133.3 1.3 copy-done.2
  134.7 2.5 shard_map.116
  137.1 15.0 %all_to_all.32.refs_1_ = f32[16,2,32,128]{3,2,1,0:T(8,128)S(1)} all-to-all(f32[16,2,32,128]{3,2,1,0:T(8,128)S(1)} %shard_map.116), channel_id=1, replica_groups=mesh['prow'=32,'pcol'=16] {'pcol'}, dimensions={0} | all-to-all | bytes 1048576 | tf_op jit(solution)/shard_map/all_to_all | solution.py:293
  152.1 0.0 copy-done.3
  152.1 0.8 shard_map.117
  152.9 18.4 %all_gather.69.refs_2_ = f32[32,32,128]{2,1,0:T(8,128)S(1)} all-gather(f32[2,32,128]{2,1,0:T(8,128)S(1)} %get-tuple-element.57.refs_6_), channel_id=1, replica_groups={{0,16,64,80,128,144,192,208,256,272,320,336,384,400,448,464},{32,48,96,..., dimensions={0}, use_global_device_ids=true | all-gather | bytes 557056 | tf_op jit(solution)/shard_map/all_gather | solution.py:290
  171.3 1.3 copy-done.7
  172.6 1.9 shard_map.118
  174.5 0.8 copy-done.11
  175.3 4.7 %all-to-all-start.3 = ((f32[16,2,32,128]{3,2,1,0:T(8,128)}), f32[16,2,32,128]{3,2,1,0:T(8,128)S(1)}, u32[]{:S(2)}, u32[]{:S(2)}) async-start(f32[16,2,32,128]{3,2,1,0:T(8,128)} %copy-done.11), calls=%async_computation.3 | async-start | bytes 1048576 | tf_op jit(solution)/shard_map/all_to_all | solution.py:293
  180.0 0.0 all-gather.22.cloned.1.call-start
  180.0 0.5 all-gather.22.cloned.1.call-update
  180.6 10.5 %all-to-all-done.3.refs_0_ = f32[16,2,32,128]{3,2,1,0:T(8,128)S(1)} async-done(((f32[16,2,32,128]{3,2,1,0:T(8,128)}), f32[16,2,32,128]{3,2,1,0:T(8,128)S(1)}, u32[]{:S(2)}, u32[]{:S(2)}) %all-to-all-start.3) | async-done | bytes 524320 | tf_op jit(solution)/shard_map/all_to_all | solution.py:293
  191.0 0.0 copy-done.8
  191.0 0.2 shard_map.119.refs_5_
  191.2 22.3 %all_gather.72.refs_2_ = f32[32,32,128]{2,1,0:T(8,128)S(1)} all-gather(f32[2,32,128]{2,1,0:T(8,128)S(1)} %shard_map.119.refs_5_), channel_id=1, replica_groups={{0,16,64,80,128,144,192,208,256,272,320,336,384,400,448,464},{32,48,96,..., dimensions={0}, use_global_device_ids=true | all-gather | bytes 557056 | tf_op jit(solution)/shard_map/all_gather | solution.py:290
  213.5 1.3 copy-done.9
  214.8 1.9 shard_map.120
  216.6 15.1 %all_to_all.33.refs_0_ = f32[16,2,32,128]{3,2,1,0:T(8,128)S(1)} all-to-all(f32[16,2,32,128]{3,2,1,0:T(8,128)S(1)} %shard_map.120), channel_id=1, replica_groups=mesh['prow'=32,'pcol'=16] {'pcol'}, dimensions={0} | all-to-all | bytes 1048576 | tf_op jit(solution)/shard_map/all_to_all | solution.py:293
  231.7 0.2 shard_map.121.refs_4_
  231.9 18.3 %all_gather.75.refs_2_ = f32[32,32,128]{2,1,0:T(8,128)S(1)} all-gather(f32[2,32,128]{2,1,0:T(8,128)S(1)} %shard_map.121.refs_4_), channel_id=1, replica_groups={{0,16,64,80,128,144,192,208,256,272,320,336,384,400,448,464},{32,48,96,..., dimensions={0}, use_global_device_ids=true | all-gather | bytes 557056 | tf_op jit(solution)/shard_map/all_gather | solution.py:290
  250.2 1.3 copy-done.5
  251.5 1.9 shard_map.122
  253.3 15.1 %all_to_all.34.refs_1_ = f32[16,2,32,128]{3,2,1,0:T(8,128)S(1)} all-to-all(f32[16,2,32,128]{3,2,1,0:T(8,128)S(1)} %shard_map.122), channel_id=1, replica_groups=mesh['prow'=32,'pcol'=16] {'pcol'}, dimensions={0} | all-to-all | bytes 1048576 | tf_op jit(solution)/shard_map/all_to_all | solution.py:293
  268.4 0.2 shard_map.123
  268.6 5.6 %all-gather.7 = f32[8,2,32,128]{3,2,1,0:T(8,128)S(1)} all-gather(f32[4,2,32,128]{3,2,1,0:T(8,128)S(1)} %shard_map.123), channel_id=9, replica_groups={{0,32},{16,48},{64,96},{80,112},{128,160},{144,176},{192,224},{208,240}..., dimensions={0}, use_global_device_ids=true | all-gather | bytes 393216 | tf_op jit(solution)/shard_map/all_gather | solution.py:287
  274.2 0.7 shard_map.124
  (17 shorter events, 0.0 us)
Async XLA Ops:
  6.5 85.3 %all-gather.14.cloned.1.call-start = ((), (), s32[]{:S(2)}) async-start(), calls=%async_computation.6 | async-start | bytes 2015232 | tf_op jit(solution)/shard_map/all_gather | solution.py:287
  37.7 95.6 %all-gather.16.cloned.1.call-start = ((), (), s32[]{:S(2)}) async-start(), calls=%async_computation.7 | async-start | bytes 2064384 | tf_op jit(solution)/shard_map/all_gather | solution.py:287
  37.7 12.3 %collective-permute-start = (f32[16,64,128]{2,1,0:T(8,128)S(1)}, f32[16,64,128]{2,1,0:T(8,128)S(1)}, u32[]{:S(2)}, u32[]{:S(2)}) collective-permute-start(f32[16,64,128]{2,1,0:T(8,128)S(1)} %bitcast.42), channel_id=1, source_target_pairs={{0,32},{16,496},{32,64},{48,16},{64,96},{80,48},{96,128},{112,80},... | collective-permute-start | bytes 1572872 | tf_op jit(solution)/shard_map/ppermute | solution.py:303
  40.7 9.3 %copy-start.4 = (f32[3,1,1,16,64,128]{5,4,3,2,1,0:T(8,128)S(1)}, f32[3,1,1,16,64,128]{5,4,3,2,1,0:T(8,128)}, u32[]{:S(2)}) copy-start(f32[3,1,1,16,64,128]{5,4,3,2,1,0:T(8,128)} %refs_6_.1) | copy-start | bytes 4718596
  40.7 9.3 %copy-start.13 = (s32[3,1,1,16,64]{4,3,2,1,0:T(8,128)S(1)}, s32[3,1,1,16,64]{4,3,2,1,0:T(8,128)}, u32[]{:S(2)}) copy-start(s32[3,1,1,16,64]{4,3,2,1,0:T(8,128)} %refs_3_.1) | copy-start | bytes 36868
  40.7 9.3 %copy-start.14 = (s32[3,1,1,16]{3,2,1,0:T(1,128)S(1)}, s32[3,1,1,16]{3,2,1,0:T(1,128)}, u32[]{:S(2)}) copy-start(s32[3,1,1,16]{3,2,1,0:T(1,128)} %refs_1_.2) | copy-start | bytes 580
  40.7 9.3 %copy-start.15 = (s32[3,1,1,16]{3,2,1,0:T(1,128)S(1)}, s32[3,1,1,16]{3,2,1,0:T(1,128)}, u32[]{:S(2)}) copy-start(s32[3,1,1,16]{3,2,1,0:T(1,128)} %refs_2_.2) | copy-start | bytes 580
  50.0 17.5 %copy-start.10 = (f32[4,1,1,128,128]{4,3,2,1,0:T(8,128)S(1)}, f32[4,1,1,128,128]{4,3,2,1,0:T(8,128)}, u32[]{:S(2)}) copy-start(f32[4,1,1,128,128]{4,3,2,1,0:T(8,128)} %refs_2_.3) | copy-start | bytes 786436
  50.0 17.5 %copy-start.12 = (f32[4,1,1,64,128]{4,3,2,1,0:T(8,128)S(1)}, f32[4,1,1,64,128]{4,3,2,1,0:T(8,128)}, u32[]{:S(2)}) copy-start(f32[4,1,1,64,128]{4,3,2,1,0:T(8,128)} %refs_1_.3) | copy-start | bytes 393220
  67.7 103.6 %all-gather.18.cloned.1.call-start = ((), (), s32[]{:S(2)}) async-start(), calls=%async_computation.8 | async-start | bytes 1769472 | tf_op jit(solution)/shard_map/all_gather | solution.py:287
  72.4 141.1 %all-gather.20.cloned.1.call-start = ((), (), s32[]{:S(2)}) async-start(), calls=%async_computation.9 | async-start | bytes 1769472 | tf_op jit(solution)/shard_map/all_gather | solution.py:287
  91.8 1.3 copy-start
  93.1 17.8 %copy-start.1 = (f32[2624,128]{1,0:T(8,128)S(1)}, f32[2624,128]{1,0:T(8,128)}, u32[]{:S(2)}) copy-start(f32[2624,128]{1,0:T(8,128)} %all-gather.14.cloned.1.call-done) | copy-start | bytes 4030468
  133.3 1.3 copy-start.2
  134.6 17.5 %copy-start.3 = (f32[2688,128]{1,0:T(8,128)S(1)}, f32[2688,128]{1,0:T(8,128)}, u32[]{:S(2)}) copy-start(f32[2688,128]{1,0:T(8,128)} %all-gather.16.cloned.1.call-done) | copy-start | bytes 4128772
  171.3 1.3 copy-start.7
  174.5 0.8 copy-start.11
  175.3 15.8 %copy-start.8 = (f32[2304,128]{1,0:T(8,128)S(1)}, f32[2304,128]{1,0:T(8,128)}, u32[]{:S(2)}) copy-start(f32[2304,128]{1,0:T(8,128)} %all-gather.18.cloned.1.call-done) | copy-start | bytes 3538948
  175.3 15.8 %all-to-all-start.3 = ((f32[16,2,32,128]{3,2,1,0:T(8,128)}), f32[16,2,32,128]{3,2,1,0:T(8,128)S(1)}, u32[]{:S(2)}, u32[]{:S(2)}) async-start(f32[16,2,32,128]{3,2,1,0:T(8,128)} %copy-done.11), calls=%async_computation.3 | async-start | bytes 1048576 | tf_op jit(solution)/shard_map/all_to_all | solution.py:293
  180.0 70.2 %all-gather.22.cloned.1.call-start = ((), (), s32[]{:S(2)}) async-start(), calls=%async_computation.10 | async-start | bytes 1867776 | tf_op jit(solution)/shard_map/all_gather | solution.py:287
  213.5 1.3 copy-start.9
  250.2 1.3 copy-start.5
  251.5 17.0 %copy-start.6 = (f32[2432,128]{1,0:T(8,128)S(1)}, f32[2432,128]{1,0:T(8,128)}, u32[]{:S(2)}) copy-start(f32[2432,128]{1,0:T(8,128)} %all-gather.22.cloned.1.call-done) | copy-start | bytes 3735556
Sparse Core Ops, SparseCore 0:
  37.8 30.9 all-gather.13
  70.8 37.0 all-gather.15
  110.0 33.4 all-gather.17
  145.5 33.8 all-gather.19
  182.6 34.0 all-gather.21
